TPU v7x, 32 devices: a whole 2x2x4 slice. The times are simulated.
32 devices in a mesh: dp: 4 (over y, x), expert: 4 (over z), tensor: 2 (over core).
Axes of the slice: x: 2, y: 2, z: 4, core: 2. Of those that a mesh axis runs over, the one named last changes fastest.
Arguments:
- weight: bfloat16 [4, 1536, 4096], P('expert', 'tensor'), may hold values from -1.796875 to 1.796875
- factor_a: float32 [4, 64, 4096], P('expert', 'dp', 'tensor'), may hold values from -1.2 to 1.2
- factor_b: float32 [4, 64, 1536], P('expert', 'dp', 'tensor'), may hold values from -1.2 to 1.2
- moment_a: float32 [4, 64, 4096], P('expert', 'dp', 'tensor'), may hold values from -0.6 to 0.6
- second_a: float32 [4, 64, 4096], P('expert', 'dp', 'tensor'), may hold values from 0.003 to 1
- first_moment_factor_b: float32 [4, 64, 1536], P('expert', 'dp', 'tensor'), may hold values from -0.6 to 0.6
- second_b: float32 [4, 64, 1536], P('expert', 'dp', 'tensor'), may hold values from 0.003 to 1
- grad_a: float32 [4, 4, 64, 4096], P('dp', 'expert', None, 'tensor'), may hold values from -2 to 2
- grad_b: float32 [4, 4, 64, 1536], P('dp', 'expert', None, 'tensor'), may hold values from -2 to 2
- slot_of: int32 [4], replicated, may hold values from 0 to 3, each once
Outputs:
- merged: bfloat16 [4, 1536, 4096], P('expert', 'tensor')
- new_a: float32 [4, 64, 4096], P('expert', 'dp', 'tensor')
- new_b: float32 [4, 64, 1536], P('expert', 'dp', 'tensor')
- new_moment_a: float32 [4, 64, 4096], P('expert', 'dp', 'tensor')
- new_second_a: float32 [4, 64, 4096], P('expert', 'dp', 'tensor')
- new_moment_b: float32 [4, 64, 1536], P('expert', 'dp', 'tensor')
- new_second_b: float32 [4, 64, 1536], P('expert', 'dp', 'tensor')
Inputs may be any that keep to these rules, and one draw needn't show every extreme that they name: slot_of is a permutation; slot s belongs to the index s // 1 of expert.
All inputs are finite; a program needn't handle non-finite values.
Results may differ from a plain program's by a relative error of at most 0.0065.
Values may be sent and summed in bfloat16 or wider, within the bound.
No kernel may reach another device: no remote copies, remote signals or barrier semaphores. Data moves between devices by JAX's collectives and lax.ppermute only.
A program may use at most 64 MiB of HBM per device.

v0:
```python
import jax
import jax.numpy as jnp
from jax import lax
from jax.sharding import PartitionSpec as P

ADAM_STEP = 20


ADAPTER_SCALE = 2.0
BETA_ONE = 0.9
BETA_TWO = 0.95
LEARN_RATE = 0.08
STABILITY_TERM = 1e-08


def adam_update(param, moment, second, grad):
    corr_one = 1.0 - BETA_ONE**ADAM_STEP
    corr_two = 1.0 - BETA_TWO**ADAM_STEP
    moment_new = BETA_ONE * moment + (1.0 - BETA_ONE) * grad
    second_new = BETA_TWO * second + (1.0 - BETA_TWO) * grad * grad
    param_new = param - LEARN_RATE * (moment_new / corr_one) / (
        jnp.sqrt(second_new / corr_two) + STABILITY_TERM
    )
    return (param_new, moment_new, second_new)


def per_device(
    weight,
    factor_a,
    factor_b,
    moment_a,
    second_a,
    first_moment_factor_b,
    second_b,
    grad_a,
    grad_b,
    slot_of,
):
    reduced_factor_a, summed_b = (
        lax.psum_scatter(grad_a.astype(jnp.bfloat16), "dp", scatter_dimension=2, tiled=True).astype(
            jnp.float32
        ),
        lax.psum_scatter(grad_b.astype(jnp.bfloat16), "dp", scatter_dimension=2, tiled=True).astype(
            jnp.float32
        ),
    )
    new_a, new_moment_a, new_second_a = adam_update(
        factor_a, moment_a, second_a, reduced_factor_a[0]
    )
    new_b, new_moment_b, new_second_b = adam_update(
        factor_b, first_moment_factor_b, second_b, summed_b[0]
    )
    send_a = new_a.astype(jnp.bfloat16)
    send_b = new_b.astype(jnp.bfloat16)
    slots_here = send_a.shape[0]
    my_slots = lax.axis_index("expert") * slots_here + jnp.arange(slots_here, dtype=jnp.int32)
    full_a, full_b = (
        lax.all_gather(send_a, "dp", axis=1, tiled=True),
        lax.all_gather(send_b, "dp", axis=1, tiled=True),
    )
    select = (slot_of[None, :] == my_slots[:, None]).astype(jnp.bfloat16)
    picked_a = jnp.einsum(
        "jk,krc->jrc",
        select,
        lax.all_gather(full_a, "expert", axis=0, tiled=True),
        preferred_element_type=jnp.float32,
    )
    picked_b = jnp.einsum(
        "jk,krc->jrc",
        select,
        lax.all_gather(full_b, "expert", axis=0, tiled=True),
        preferred_element_type=jnp.float32,
    )
    rows_a = picked_a.astype(jnp.bfloat16)
    rows_b = picked_b.astype(jnp.bfloat16)
    weight_increment = jnp.einsum(
        "jrf,jrc->jfc",
        rows_b,
        lax.all_gather(rows_a, "tensor", axis=2, tiled=True),
        preferred_element_type=jnp.float32,
    )
    merged = (weight.astype(jnp.float32) + ADAPTER_SCALE * weight_increment).astype(jnp.bfloat16)
    return (merged, new_a, new_b, new_moment_a, new_second_a, new_moment_b, new_second_b)


def solution(mesh):
    in_specs = (
        P("expert", "tensor", None),
        P("expert", "dp", "tensor"),
        P("expert", "dp", "tensor"),
        P("expert", "dp", "tensor"),
        P("expert", "dp", "tensor"),
        P("expert", "dp", "tensor"),
        P("expert", "dp", "tensor"),
        P("dp", "expert", None, "tensor"),
        P("dp", "expert", None, "tensor"),
        P(),
    )
    out_specs = (
        P("expert", "tensor", None),
        P("expert", "dp", "tensor"),
        P("expert", "dp", "tensor"),
        P("expert", "dp", "tensor"),
        P("expert", "dp", "tensor"),
        P("expert", "dp", "tensor"),
        P("expert", "dp", "tensor"),
    )
    return jax.shard_map(
        per_device, mesh=mesh, in_specs=in_specs, out_specs=out_specs, check_vma=False
    )
```

profile of v0, /device:TPU:1, one launch (start us, length us, event | category | flops | bytes accessed | tf_op | source)
XLA Modules:
  0.0 118.8 jit_solution(2085421200078512574)
XLA Ops:
  7.2 0.0 reduce-scatter.5.cloned.1.call-start
  7.2 1.8 %convert_element_type.35 = bf16[1,1,64,2048]{3,2,1,0:T(8,128)(2,1)} convert(f32[1,1,64,2048]{3,2,1,0:T(8,128)} %param.17) | non-fusion elementwise | flops 131072 | bytes 786432 | tf_op jit(solution)/shard_map/convert_element_type | solution.py:40
  9.0 0.0 reduce-scatter.5.cloned.1.call-update
  9.0 0.0 reduce-scatter.3.cloned.1.call-start
  9.1 1.6 %convert_element_type.32 = bf16[1,1,64,768]{3,2,1,0:T(8,128)(2,1)} convert(f32[1,1,64,768]{3,2,1,0:T(8,128)} %param.18) | non-fusion elementwise | flops 49152 | bytes 294912 | tf_op jit(solution)/shard_map/convert_element_type | solution.py:43
  10.6 0.0 reduce-scatter.3.cloned.1.call-update
  10.7 0.0 all-gather.3.cloned.1.call-start
  10.7 26.3 %reduce-scatter.5.cloned.1.call-done = bf16[1,1,16,2048]{3,2,1,0:T(8,128)(2,1)} async-done(((bf16[1,1,64,2048]{3,2,1,0:T(8,128)(2,1)}), bf16[1,1,16,2048]{3,2,1,0:T(8,128)(2,1)}) %reduce-scatter.5.cloned.1.call-update) | async-done | bytes 65552 | tf_op jit(solution)/shard_map/reduce_scatter | solution.py:40
  37.0 1.9 %fusion.12 = (bf16[1,16,2048]{2,1,0:T(8,128)(2,1)S(1)}, f32[1,16,2048]{2,1,0:T(8,128)}, f32[1,16,2048]{2,1,0:T(8,128)}, f32[1,16,2048]{2,1,0:T(8,128)}) fusion(f32[1,16,2048]{2,1,0:T(8,128)} %param.11, bf16[1,1,16,2048]{3,2,1,0:T(8,128)(2,1)} %reduce-scatter.5.cloned.1.call-done, f32[1,16,2048]{2,1,0:T(8,128)} %param.13, f32[1,16,2048]{2,1,0:T(8,128)} %param.14), kind=kLoop, calls=%fused_computation.22 | loop fusion | flops 458752 | bytes 917504 | tf_op jit(solution)/shard_map/convert_element_type | solution.py:53
  38.9 7.5 %all_gather.17 = bf16[1,64,2048]{2,1,0:T(8,128)(2,1)} all-gather(bf16[1,16,2048]{2,1,0:T(8,128)(2,1)S(1)} %get-tuple-element.11), channel_id=1, replica_groups=mesh['dp'=4,'expert'=4,'tensor'=2] {'dp'}, dimensions={1}, use_global_device_ids=true | all-gather | bytes 327680 | tf_op jit(solution)/shard_map/all_gather | solution.py:58
  46.4 0.0 all-gather.3.cloned.1.call-update
  46.5 17.4 %reduce-scatter.3.cloned.1.call-done = bf16[1,1,16,768]{3,2,1,0:T(8,128)(2,1)} async-done(((bf16[1,1,64,768]{3,2,1,0:T(8,128)(2,1)}), bf16[1,1,16,768]{3,2,1,0:T(8,128)(2,1)}) %reduce-scatter.3.cloned.1.call-update) | async-done | bytes 24592 | tf_op jit(solution)/shard_map/reduce_scatter | solution.py:43
  63.8 1.5 %fusion.9 = (bf16[1,16,768]{2,1,0:T(8,128)(2,1)S(1)}, f32[1,16,768]{2,1,0:T(8,128)}, f32[1,16,768]{2,1,0:T(8,128)}, f32[1,16,768]{2,1,0:T(8,128)}) fusion(f32[1,16,768]{2,1,0:T(8,128)} %param.12, bf16[1,1,16,768]{3,2,1,0:T(8,128)(2,1)} %reduce-scatter.3.cloned.1.call-done, f32[1,16,768]{2,1,0:T(8,128)} %param.15, f32[1,16,768]{2,1,0:T(8,128)} %param.16), kind=kLoop, calls=%fused_computation.21 | loop fusion | flops 172032 | bytes 344064 | tf_op jit(solution)/shard_map/convert_element_type | solution.py:54
  65.4 6.3 %all_gather.15 = bf16[1,64,768]{2,1,0:T(8,128)(2,1)S(1)} all-gather(bf16[1,16,768]{2,1,0:T(8,128)(2,1)S(1)} %get-tuple-element.7), channel_id=1, replica_groups=mesh['dp'=4,'expert'=4,'tensor'=2] {'dp'}, dimensions={1}, use_global_device_ids=true | all-gather | bytes 122880 | tf_op jit(solution)/shard_map/all_gather | solution.py:59
  71.7 17.1 %all_gather.16 = bf16[4,64,768]{2,1,0:T(8,128)(2,1)S(1)} all-gather(bf16[1,64,768]{2,1,0:T(8,128)(2,1)S(1)} %all_gather.15), channel_id=1, replica_groups=mesh['dp'=4,'expert'=4,'tensor'=2] {'expert'}, dimensions={0}, use_global_device_ids=true | all-gather | bytes 491520 | tf_op jit(solution)/shard_map/all_gather | solution.py:71
  88.8 1.1 fusion.3
  89.8 10.5 %all-gather.3.cloned.1.call-done = bf16[4,64,2048]{2,1,0:T(8,128)(2,1)} async-done(((bf16[1,64,2048]{2,1,0:T(8,128)(2,1)}), bf16[4,64,2048]{2,1,0:T(8,128)(2,1)}) %all-gather.3.cloned.1.call-update) | async-done | bytes 1048592 | tf_op jit(solution)/shard_map/all_gather | solution.py:65
  100.4 2.1 %fusion.1 = bf16[1,64,2048]{2,0,1:T(2,128)(2,1)S(1)} fusion(bf16[4,64,2048]{2,1,0:T(8,128)(2,1)} %all-gather.3.cloned.1.call-done, s32[4]{0:T(128)} %param.19, s32[]{:T(128)S(6)} %axis_index.15), kind=kOutput, calls=%fused_computation.2 | convolution fusion | flops 1048580 | bytes 1310740 | tf_op jit(solution)/shard_map/jk,krc->jrc/dot_general | solution.py:62
  102.5 0.2 copy.28
  102.6 2.3 %all-gather = bf16[64,4096]{1,0:T(8,128)(2,1)S(1)} all-gather(bf16[64,2048]{1,0:T(8,128)(2,1)S(1)} %bitcast.28), channel_id=2, replica_groups=mesh['dp'=4,'expert'=4,'tensor'=2] {'tensor'}, dimensions={1}, use_global_device_ids=true | all-gather | bytes 786432 | tf_op jit(solution)/shard_map/all_gather | solution.py:79
  104.9 7.3 %fusion = bf16[1,768,4096]{2,1,0:T(8,128)(2,1)} fusion(bf16[1,768,4096]{2,1,0:T(8,128)(2,1)} %param.10, bf16[64,4096]{1,0:T(8,128)(2,1)S(1)} %all-gather, bf16[1,64,768]{2,0,1:T(2,128)(2,1)S(1)} %fusion.3), kind=kOutput, calls=%fused_computation.1 | convolution fusion | flops 415236096 | bytes 13205504 | tf_op jit(solution)/shard_map/jrf,jrc->jfc/dot_general | solution.py:76
Async XLA Ops:
  7.2 29.9 %reduce-scatter.5.cloned.1.call-start = ((), (), s32[]{:S(2)}) async-start(), calls=%async_computation.3 | async-start | bytes 327680 | tf_op jit(solution)/shard_map/reduce_scatter | solution.py:40
  9.0 54.8 %reduce-scatter.3.cloned.1.call-start = ((), (), s32[]{:S(2)}) async-start(), calls=%async_computation.2 | async-start | bytes 122880 | tf_op jit(solution)/shard_map/reduce_scatter | solution.py:43
  10.7 89.7 %all-gather.3.cloned.1.call-start = ((), (), s32[]{:S(2)}) async-start(), calls=%async_computation.4 | async-start | bytes 1310720 | tf_op jit(solution)/shard_map/all_gather | solution.py:65
Sparse Core Ops, SparseCore 0:
  11.3 25.6 reduce-scatter.4
  40.0 23.8 reduce-scatter.2
  65.4 34.9 all-gather.2
where the time goes:
time: 119 us
  waiting for transfers between devices  54.3 us (46%)
  blocking collectives  33.2 us (28%)
  between operations  13.8 us (12%)
  matrix products  10.5 us (9%)
  other arithmetic  6.74 us (6%)
    reduce_scatter x1, waiting for transfers between devices, per_device(): lax.psum_scatter(grad_a.astype(jnp.bfloat16), 'dp', scatter_dimension=2,...  26.3 us
    reduce_scatter x1, waiting for transfers between devices, per_device(): lax.psum_scatter(grad_b.astype(jnp.bfloat16), 'dp', scatter_dimension=2,...  17.4 us
    all_gather x1, blocking collectives, per_device(): lax.all_gather(full_b, 'expert', axis=0, tiled=True)  17.1 us
    all_gather x1, waiting for transfers between devices, per_device(): lax.all_gather(full_a, 'expert', axis=0, tiled=True)  10.5 us
    all_gather x1, blocking collectives, per_device(): lax.all_gather(send_a, 'dp', axis=1, tiled=True)  7.53 us
    dot_general x1, matrix products, per_device(): jnp.einsum('jrf,jrc->jfc', rows_b, lax.all_gather(rows_a, 'tensor', axis=...  7.31 us
    all_gather x1, blocking collectives, per_device(): lax.all_gather(send_b, 'dp', axis=1, tiled=True)  6.3 us
  transfers between devices with their start and end apart: 3, of which 3 were waited for; matrix products, arithmetic and copies ran while one was open for 5% of the time, Pallas kernels for 0%

commit v1 on v0

v1 whole, which is shorter than its diff:
```python
import jax
import jax.numpy as jnp
from jax import lax
from jax.sharding import PartitionSpec as P

ADAM_STEP = 20


ADAPTER_SCALE = 2.0
BETA_ONE = 0.9
BETA_TWO = 0.95
LEARN_RATE = 0.08
STABILITY_TERM = 1e-08


def adam_update(param, moment, second, grad):
    corr_one = 1.0 - BETA_ONE**ADAM_STEP
    corr_two = 1.0 - BETA_TWO**ADAM_STEP
    moment_new = BETA_ONE * moment + (1.0 - BETA_ONE) * grad
    second_new = BETA_TWO * second + (1.0 - BETA_TWO) * grad * grad
    param_new = param - LEARN_RATE * (moment_new / corr_one) / (
        jnp.sqrt(second_new / corr_two) + STABILITY_TERM
    )
    return (param_new, moment_new, second_new)


def swap(x, axis, n, k):
    return lax.ppermute(x, axis, [(i, i ^ k) for i in range(n)])


def per_device(
    n_dp,
    n_expert,
    n_tensor,
    weight,
    factor_a,
    factor_b,
    moment_a,
    second_a,
    first_moment_factor_b,
    second_b,
    grad_a,
    grad_b,
    slot_of,
):
    ranks = factor_a.shape[1]
    cols_a = factor_a.shape[2]
    me = lax.axis_index("dp")
    here = lax.axis_index("expert")

    def rows_of(k):
        start = (me ^ k) * ranks
        return (
            lax.dynamic_slice_in_dim(grad_a[0, 0], start, ranks, 0),
            lax.dynamic_slice_in_dim(grad_b[0, 0], start, ranks, 0),
        )

    summed_a, summed_b = rows_of(0)
    got = []
    for k in range(1, n_dp):
        piece = jnp.concatenate(rows_of(k), axis=1).astype(jnp.bfloat16)
        got.append(swap(piece, "dp", n_dp, k))
    for piece in got:
        summed_a = summed_a + piece[:, :cols_a].astype(jnp.float32)
        summed_b = summed_b + piece[:, cols_a:].astype(jnp.float32)

    new_a, new_moment_a, new_second_a = adam_update(factor_a, moment_a, second_a, summed_a[None])
    new_b, new_moment_b, new_second_b = adam_update(
        factor_b, first_moment_factor_b, second_b, summed_b[None]
    )
    send = jnp.concatenate([new_a[0], new_b[0]], axis=1).astype(jnp.bfloat16)

    experts = jnp.arange(n_expert, dtype=jnp.int32)
    wanted = jnp.sum(jnp.where(slot_of == here, experts, 0)) ^ here
    mine = send
    others = [swap(send, "expert", n_expert, k) for k in range(1, n_expert)]
    for k, piece in enumerate(others, 1):
        mine = jnp.where(wanted == k, piece, mine)

    parts = [mine] + [swap(mine, "dp", n_dp, k) for k in range(1, n_dp)]
    rows_a = jnp.concatenate([p[:, :cols_a] for p in parts], axis=0)
    rows_b = jnp.concatenate([p[:, cols_a:] for p in parts], axis=0)
    full_a = lax.all_gather(rows_a, "tensor", axis=1, tiled=True)
    increment = jnp.einsum("rf,rc->fc", rows_b, full_a, preferred_element_type=jnp.float32)
    merged = (weight[0].astype(jnp.float32) + ADAPTER_SCALE * increment).astype(jnp.bfloat16)
    return (merged[None], new_a, new_b, new_moment_a, new_second_a, new_moment_b, new_second_b)


def solution(mesh):
    sizes = dict(mesh.shape)

    def body(*args):
        return per_device(sizes["dp"], sizes["expert"], sizes["tensor"], *args)

    state = P("expert", "dp", "tensor")
    grad = P("dp", "expert", None, "tensor")
    weight = P("expert", "tensor", None)
    in_specs = (weight,) + (state,) * 6 + (grad,) * 2 + (P(),)
    out_specs = (weight,) + (state,) * 6
    return jax.shard_map(body, mesh=mesh, in_specs=in_specs, out_specs=out_specs, check_vma=False)
```

time: 119 us -> 43.2 us (0.36)
  waiting for transfers between devices: 54.3 us -> 10.8 us
  blocking collectives: 33.2 us -> 6.43 us
  between operations: 13.8 us -> 1.38 us
  starting transfers between devices: 0.12 us -> 9.88 us
  matrix products: 10.5 us -> 7.32 us
  other arithmetic: 6.74 us -> 4.85 us
  local copies, waits for them, and re-layouts: 0.15 us -> 1.96 us
    reduce_scatter x2 -> x0, waiting for transfers between devices: 43.7 us -> none  [the longest x1 26.3 us: per_device(): lax.psum_scatter(grad_a.astype(jnp.bfloat16), 'dp', scatter_dimension=2,...]
    all_gather x4 -> x1, blocking collectives: 33.2 us -> 6.43 us  [per_device(): full_a = lax.all_gather(rows_a, 'tensor', axis=1, tiled=True)]
    ppermute x0 -> x9, waiting for transfers between devices: none -> 10.8 us  [swap(): return lax.ppermute(x, axis, [(i, i ^ k) for i in range(n)])]
    all_gather x1 -> x0, waiting for transfers between devices: 10.5 us -> none  [per_device(): lax.all_gather(full_a, 'expert', axis=0, tiled=True)]
    ppermute x0 -> x9, starting transfers between devices: none -> 9.88 us  [swap(): return lax.ppermute(x, axis, [(i, i ^ k) for i in range(n)])]
    convert_element_type x4 -> x0, other arithmetic: 6.74 us -> none  [the longest x1 1.86 us: per_device(): send_a = new_a.astype(jnp.bfloat16)]
    squeeze x0 -> x2, other arithmetic: none -> 3.45 us  [per_device(): send = jnp.concatenate([new_a[0], new_b[0]], axis=1).astype(jnp.bfloat16)]
    dot_general x3 -> x1, matrix products: 10.5 us -> 7.32 us  [per_device(): jnp.einsum('rf,rc->fc', rows_b, full_a, preferred_element_type=jnp.float32)]
  transfers between devices with their start and end apart: 3 -> 9, of which waited for: 3 -> 7; matrix products, arithmetic and copies ran while one was open for 5% -> 3% of each run, Pallas kernels for 0% -> 0%
where the time goes in v1:
time: 43.2 us; the launch traced here: 42.6 us
  waiting for transfers between devices  10.8 us (25%)
  starting transfers between devices  9.88 us (23%)
  matrix products  7.32 us (17%)
  blocking collectives  6.43 us (15%)
  other arithmetic  4.85 us (11%)
  local copies, waits for them, and re-layouts  1.96 us (5%)
  between operations  1.38 us (3%)
    ppermute x9, waiting for transfers between devices, swap(): return lax.ppermute(x, axis, [(i, i ^ k) for i in range(n)])  10.8 us
    ppermute x9, starting transfers between devices, swap(): return lax.ppermute(x, axis, [(i, i ^ k) for i in range(n)])  9.88 us
    dot_general x1, matrix products, per_device(): jnp.einsum('rf,rc->fc', rows_b, full_a, preferred_element_type=jnp.float32)  7.32 us
    all_gather x1, blocking collectives, per_device(): full_a = lax.all_gather(rows_a, 'tensor', axis=1, tiled=True)  6.43 us
    squeeze x2, other arithmetic, per_device(): send = jnp.concatenate([new_a[0], new_b[0]], axis=1).astype(jnp.bfloat16)  3.45 us
    reduce_sum x1, other arithmetic, per_device(): wanted = jnp.sum(jnp.where(slot_of == here, experts, 0)) ^ here  1.29 us
    dynamic_slice x1, local copies, waits for them, and re-layouts, rows_of(): lax.dynamic_slice_in_dim(grad_a[0, 0], start, ranks, 0)  1.06 us
    dynamic_slice x1, local copies, waits for them, and re-layouts, rows_of(): lax.dynamic_slice_in_dim(grad_b[0, 0], start, ranks, 0)  0.86 us
  transfers between devices with their start and end apart: 9, of which 7 were waited for; matrix products, arithmetic and copies ran while one was open for 3% of the time, Pallas kernels for 0%

profile of v1, /device:TPU:1, one launch (start us, length us, event | category | flops | bytes accessed | tf_op | source)
XLA Modules:
  0.0 42.6 jit_solution(14550628563556484845)
XLA Ops:
  0.7 0.9 %fusion.20 = (bf16[16,768]{1,0:T(8,128)(2,1)S(1)}, bf16[16,768]{1,0:T(8,128)(2,1)S(1)}, bf16[16,768]{1,0:T(8,128)(2,1)S(1)}) fusion(f32[1,1,64,768]{3,2,1,0:T(8,128)} %param.18, s32[]{:T(128)S(6)} %select_n.43, s32[]{:T(128)S(6)} %select_n.44, s32[]{:T(128)S(6)} %select_n.45), kind=kLoop, calls=%fused_computation.42 | loop fusion | bytes 147468 | tf_op jit(solution)/shard_map/dynamic_slice | solution.py:55
  1.5 1.1 %fusion.13 = (bf16[16,2048]{1,0:T(8,128)(2,1)S(1)}, bf16[16,2048]{1,0:T(8,128)(2,1)S(1)}, bf16[16,2048]{1,0:T(8,128)(2,1)S(1)}) fusion(f32[1,1,64,2048]{3,2,1,0:T(8,128)} %param.17, s32[]{:T(128)S(6)} %select_n.43, s32[]{:T(128)S(6)} %select_n.45, s32[]{:T(128)S(6)} %select_n.44), kind=kLoop, calls=%fused_computation.28 | loop fusion | bytes 393228 | tf_op jit(solution)/shard_map/dynamic_slice | solution.py:54
  2.6 2.1 %collective-permute-start.1 = (bf16[16,2816]{1,0:T(8,128)(2,1)S(1)}, bf16[16,2816]{1,0:T(8,128)(2,1)S(1)}, u32[]{:S(2)}, u32[]{:S(2)}) collective-permute-start(bf16[16,2816]{1,0:T(8,128)(2,1)S(1)} %pad_maximum_fusion.2), channel_id=1, source_target_pairs={{0,16},{8,24},{16,0},{24,8},{1,17},{9,25},{17,1},{25,9},{2,18},{10... | collective-permute-start | bytes 270344 | tf_op jit(solution)/shard_map/ppermute | solution.py:28
  4.7 1.2 %collective-permute-start.2 = (bf16[16,2816]{1,0:T(8,128)(2,1)S(1)}, bf16[16,2816]{1,0:T(8,128)(2,1)S(1)}, u32[]{:S(2)}, u32[]{:S(2)}) collective-permute-start(bf16[16,2816]{1,0:T(8,128)(2,1)S(1)} %pad_maximum_fusion.3), channel_id=1, source_target_pairs={{0,24},{8,16},{16,8},{24,0},{1,25},{9,17},{17,9},{25,1},{2,26},{10... | collective-permute-start | bytes 270344 | tf_op jit(solution)/shard_map/ppermute | solution.py:28
  5.9 0.2 collective-permute-start
  6.1 1.0 %collective-permute-done.1 = bf16[16,2816]{1,0:T(8,128)(2,1)S(1)} collective-permute-done((bf16[16,2816]{1,0:T(8,128)(2,1)S(1)}, bf16[16,2816]{1,0:T(8,128)(2,1)S(1)}, u32[]{:S(2)}, u32[]{:S(2)}) %collective-permute-start.1) | collective-permute-done | bytes 90144 | tf_op jit(solution)/shard_map/ppermute | solution.py:28
  7.1 1.9 %collective-permute-done.2 = bf16[16,2816]{1,0:T(8,128)(2,1)S(1)} collective-permute-done((bf16[16,2816]{1,0:T(8,128)(2,1)S(1)}, bf16[16,2816]{1,0:T(8,128)(2,1)S(1)}, u32[]{:S(2)}, u32[]{:S(2)}) %collective-permute-start.2) | collective-permute-done | bytes 90144 | tf_op jit(solution)/shard_map/ppermute | solution.py:28
  9.0 1.3 %collective-permute-done = bf16[16,2816]{1,0:T(8,128)(2,1)S(1)} collective-permute-done((bf16[16,2816]{1,0:T(8,128)(2,1)S(1)}, bf16[16,2816]{1,0:T(8,128)(2,1)S(1)}, u32[]{:S(2)}, u32[]{:S(2)}) %collective-permute-start) | collective-permute-done | bytes 90144 | tf_op jit(solution)/shard_map/ppermute | solution.py:28
  10.3 1.5 %convert_bitcast_fusion.1 = (bf16[16,768]{1,0:T(8,128)(2,1)S(1)}, f32[1,16,768]{2,1,0:T(8,128)}, f32[1,16,768]{2,1,0:T(8,128)}, f32[1,16,768]{2,1,0:T(8,128)}) fusion(f32[1,16,768]{2,1,0:T(8,128)} %param.12, bf16[16,2816]{1,0:T(8,128)(2,1)S(1)} %collective-permute-done.2, bf16[16,2816]{1,0:T(8,128)(2,1)S(1)} %collective-permute-done.1, ...), kind=kLoop, calls=%fused_computation.45 | loop fusion | flops 233472 | bytes 442372 | tf_op jit(solution)/shard_map/squeeze | solution.py:71
  11.9 1.9 %convert_bitcast_fusion = (bf16[16,2048]{1,0:T(8,128)(2,1)S(1)}, f32[1,16,2048]{2,1,0:T(8,128)}, f32[1,16,2048]{2,1,0:T(8,128)}, f32[1,16,2048]{2,1,0:T(8,128)}) fusion(f32[1,16,2048]{2,1,0:T(8,128)} %param.11, bf16[16,2816]{1,0:T(8,128)(2,1)S(1)} %collective-permute-done.2, bf16[16,2816]{1,0:T(8,128)(2,1)S(1)} %collective-permute-done.1, ...), kind=kLoop, calls=%fused_computation.31 | loop fusion | flops 622592 | bytes 1179652 | tf_op jit(solution)/shard_map/squeeze | solution.py:71
  13.8 1.4 %collective-permute-start.5 = (bf16[16,2816]{1,0:T(8,128)(2,1)S(1)}, bf16[16,2816]{1,0:T(8,128)(2,1)S(1)}, u32[]{:S(2)}, u32[]{:S(2)}) collective-permute-start(bf16[16,2816]{1,0:T(8,128)(2,1)S(1)} %pad_maximum_fusion.4), channel_id=1, source_target_pairs={{0,2},{2,0},{4,6},{6,4},{1,3},{3,1},{5,7},{7,5},{8,10},{10,8},{12,... | collective-permute-start | bytes 270344 | tf_op jit(solution)/shard_map/ppermute | solution.py:28
  15.2 2.3 %collective-permute-start.4 = (bf16[16,2816]{1,0:T(8,128)(2,1)S(1)}, bf16[16,2816]{1,0:T(8,128)(2,1)S(1)}, u32[]{:S(2)}, u32[]{:S(2)}) collective-permute-start(bf16[16,2816]{1,0:T(8,128)(2,1)S(1)} %pad_maximum_fusion.4), channel_id=1, source_target_pairs={{0,4},{2,6},{4,0},{6,2},{1,5},{3,7},{5,1},{7,3},{8,12},{10,14},{12... | collective-permute-start | bytes 270344 | tf_op jit(solution)/shard_map/ppermute | solution.py:28
  17.5 0.0 collective-permute-start.3
  17.5 1.3 %fusion.23 = s32[]{:T(128)} fusion(s32[4]{0:T(128)} %param.19, s32[]{:T(128)S(6)} %axis_index.25), kind=kLoop, calls=%fused_computation.47 | loop fusion | flops 11 | bytes 24 | tf_op jit(solution)/shard_map/reduce_sum | solution.py:74
  19.5 0.0 collective-permute-done.5
  19.5 1.0 %collective-permute-done.4 = bf16[16,2816]{1,0:T(8,128)(2,1)S(1)} collective-permute-done((bf16[16,2816]{1,0:T(8,128)(2,1)S(1)}, bf16[16,2816]{1,0:T(8,128)(2,1)S(1)}, u32[]{:S(2)}, u32[]{:S(2)}) %collective-permute-start.4) | collective-permute-done | bytes 90144 | tf_op jit(solution)/shard_map/ppermute | solution.py:28
  20.4 2.9 %collective-permute-done.3 = bf16[16,2816]{1,0:T(8,128)(2,1)S(1)} collective-permute-done((bf16[16,2816]{1,0:T(8,128)(2,1)S(1)}, bf16[16,2816]{1,0:T(8,128)(2,1)S(1)}, u32[]{:S(2)}, u32[]{:S(2)}) %collective-permute-start.3) | collective-permute-done | bytes 90144 | tf_op jit(solution)/shard_map/ppermute | solution.py:28
  23.3 0.1 select_select_fusion
  23.4 2.0 %collective-permute-start.8 = (bf16[16,2816]{1,0:T(8,128)(2,1)S(1)}, bf16[16,2816]{1,0:T(8,128)(2,1)S(1)}, u32[]{:S(2)}, u32[]{:S(2)}) collective-permute-start(bf16[16,2816]{1,0:T(8,128)(2,1)S(1)} %select_select_fusion), channel_id=1, source_target_pairs={{0,24},{8,16},{16,8},{24,0},{1,25},{9,17},{17,9},{25,1},{2,26},{10... | collective-permute-start | bytes 270344 | tf_op jit(solution)/shard_map/ppermute | solution.py:28
  25.4 0.0 collective-permute-start.7
  25.4 0.7 %collective-permute-start.6 = (bf16[16,2816]{1,0:T(8,128)(2,1)S(1)}, bf16[16,2816]{1,0:T(8,128)(2,1)S(1)}, u32[]{:S(2)}, u32[]{:S(2)}) collective-permute-start(bf16[16,2816]{1,0:T(8,128)(2,1)S(1)} %select_select_fusion), channel_id=1, source_target_pairs={{0,8},{8,0},{16,24},{24,16},{1,9},{9,1},{17,25},{25,17},{2,10},{10... | collective-permute-start | bytes 270344 | tf_op jit(solution)/shard_map/ppermute | solution.py:28
  26.1 1.6 %collective-permute-done.8 = bf16[16,2816]{1,0:T(8,128)(2,1)S(1)} collective-permute-done((bf16[16,2816]{1,0:T(8,128)(2,1)S(1)}, bf16[16,2816]{1,0:T(8,128)(2,1)S(1)}, u32[]{:S(2)}, u32[]{:S(2)}) %collective-permute-start.8) | collective-permute-done | bytes 90144 | tf_op jit(solution)/shard_map/ppermute | solution.py:28
  27.7 1.0 %collective-permute-done.7 = bf16[16,2816]{1,0:T(8,128)(2,1)S(1)} collective-permute-done((bf16[16,2816]{1,0:T(8,128)(2,1)S(1)}, bf16[16,2816]{1,0:T(8,128)(2,1)S(1)}, u32[]{:S(2)}, u32[]{:S(2)}) %collective-permute-start.7) | collective-permute-done | bytes 90144 | tf_op jit(solution)/shard_map/ppermute | solution.py:28
  28.8 0.0 collective-permute-done.6
  28.8 6.4 %all_gather.3 = bf16[64,4096]{1,0:T(8,128)(2,1)S(1)} all-gather(bf16[64,2048]{1,0:T(8,128)(2,1)S(1)} %pad_maximum_fusion), channel_id=1, replica_groups=mesh['dp'=4,'expert'=4,'tensor'=2] {'tensor'}, dimensions={1}, use_global_device_ids=true | all-gather | bytes 786432 | tf_op jit(solution)/shard_map/all_gather | solution.py:83
  35.2 7.3 %fusion.1 = bf16[1,768,4096]{2,1,0:T(8,128)(2,1)} fusion(bf16[64,4096]{1,0:T(8,128)(2,1)S(1)} %all_gather.3, bf16[1,768,4096]{2,1,0:T(8,128)(2,1)} %param.10, bf16[16,768]{1,0:T(8,128)(2,1)S(1)} %slice.65, bf16[16,768]{1,0:T(8,128)(2,1)S(1)} %slice.64, bf16[16,768]{1,0:T(8,128)(2,1)S(1)} %slice.63, bf16[16,768]{1,0:T(8,128)(2,1)S(1)} %slice.62), kind=kOutput, calls=%fused_computation.2 | convolution fusion | flops 415629312 | bytes 13205504 | tf_op jit(solution)/shard_map/rf,rc->fc/dot_general | solution.py:84
  (13 shorter events, 0.1 us)
Async XLA Ops:
  2.6 4.5 %collective-permute-start.1 = (bf16[16,2816]{1,0:T(8,128)(2,1)S(1)}, bf16[16,2816]{1,0:T(8,128)(2,1)S(1)}, u32[]{:S(2)}, u32[]{:S(2)}) collective-permute-start(bf16[16,2816]{1,0:T(8,128)(2,1)S(1)} %pad_maximum_fusion.2), channel_id=1, source_target_pairs={{0,16},{8,24},{16,0},{24,8},{1,17},{9,25},{17,1},{25,9},{2,18},{10... | collective-permute-start | bytes 270344 | tf_op jit(solution)/shard_map/ppermute | solution.py:28
  4.7 4.3 %collective-permute-start.2 = (bf16[16,2816]{1,0:T(8,128)(2,1)S(1)}, bf16[16,2816]{1,0:T(8,128)(2,1)S(1)}, u32[]{:S(2)}, u32[]{:S(2)}) collective-permute-start(bf16[16,2816]{1,0:T(8,128)(2,1)S(1)} %pad_maximum_fusion.3), channel_id=1, source_target_pairs={{0,24},{8,16},{16,8},{24,0},{1,25},{9,17},{17,9},{25,1},{2,26},{10... | collective-permute-start | bytes 270344 | tf_op jit(solution)/shard_map/ppermute | solution.py:28
  5.9 4.4 %collective-permute-start = (bf16[16,2816]{1,0:T(8,128)(2,1)S(1)}, bf16[16,2816]{1,0:T(8,128)(2,1)S(1)}, u32[]{:S(2)}, u32[]{:S(2)}) collective-permute-start(bf16[16,2816]{1,0:T(8,128)(2,1)S(1)} %pad_maximum_fusion.1), channel_id=1, source_target_pairs={{0,8},{8,0},{16,24},{24,16},{1,9},{9,1},{17,25},{25,17},{2,10},{10... | collective-permute-start | bytes 270344 | tf_op jit(solution)/shard_map/ppermute | solution.py:28
  13.8 5.7 %collective-permute-start.5 = (bf16[16,2816]{1,0:T(8,128)(2,1)S(1)}, bf16[16,2816]{1,0:T(8,128)(2,1)S(1)}, u32[]{:S(2)}, u32[]{:S(2)}) collective-permute-start(bf16[16,2816]{1,0:T(8,128)(2,1)S(1)} %pad_maximum_fusion.4), channel_id=1, source_target_pairs={{0,2},{2,0},{4,6},{6,4},{1,3},{3,1},{5,7},{7,5},{8,10},{10,8},{12,... | collective-permute-start | bytes 270344 | tf_op jit(solution)/shard_map/ppermute | solution.py:28
  15.2 5.2 %collective-permute-start.4 = (bf16[16,2816]{1,0:T(8,128)(2,1)S(1)}, bf16[16,2816]{1,0:T(8,128)(2,1)S(1)}, u32[]{:S(2)}, u32[]{:S(2)}) collective-permute-start(bf16[16,2816]{1,0:T(8,128)(2,1)S(1)} %pad_maximum_fusion.4), channel_id=1, source_target_pairs={{0,4},{2,6},{4,0},{6,2},{1,5},{3,7},{5,1},{7,3},{8,12},{10,14},{12... | collective-permute-start | bytes 270344 | tf_op jit(solution)/shard_map/ppermute | solution.py:28
  17.5 5.8 %collective-permute-start.3 = (bf16[16,2816]{1,0:T(8,128)(2,1)S(1)}, bf16[16,2816]{1,0:T(8,128)(2,1)S(1)}, u32[]{:S(2)}, u32[]{:S(2)}) collective-permute-start(bf16[16,2816]{1,0:T(8,128)(2,1)S(1)} %pad_maximum_fusion.4), channel_id=1, source_target_pairs={{0,6},{2,4},{4,2},{6,0},{1,7},{3,5},{5,3},{7,1},{8,14},{10,12},{12... | collective-permute-start | bytes 270344 | tf_op jit(solution)/shard_map/ppermute | solution.py:28
  23.4 4.3 %collective-permute-start.8 = (bf16[16,2816]{1,0:T(8,128)(2,1)S(1)}, bf16[16,2816]{1,0:T(8,128)(2,1)S(1)}, u32[]{:S(2)}, u32[]{:S(2)}) collective-permute-start(bf16[16,2816]{1,0:T(8,128)(2,1)S(1)} %select_select_fusion), channel_id=1, source_target_pairs={{0,24},{8,16},{16,8},{24,0},{1,25},{9,17},{17,9},{25,1},{2,26},{10... | collective-permute-start | bytes 270344 | tf_op jit(solution)/shard_map/ppermute | solution.py:28
  25.4 3.4 %collective-permute-start.7 = (bf16[16,2816]{1,0:T(8,128)(2,1)S(1)}, bf16[16,2816]{1,0:T(8,128)(2,1)S(1)}, u32[]{:S(2)}, u32[]{:S(2)}) collective-permute-start(bf16[16,2816]{1,0:T(8,128)(2,1)S(1)} %select_select_fusion), channel_id=1, source_target_pairs={{0,16},{8,24},{16,0},{24,8},{1,17},{9,25},{17,1},{25,9},{2,18},{10... | collective-permute-start | bytes 270344 | tf_op jit(solution)/shard_map/ppermute | solution.py:28
  25.4 3.4 %collective-permute-start.6 = (bf16[16,2816]{1,0:T(8,128)(2,1)S(1)}, bf16[16,2816]{1,0:T(8,128)(2,1)S(1)}, u32[]{:S(2)}, u32[]{:S(2)}) collective-permute-start(bf16[16,2816]{1,0:T(8,128)(2,1)S(1)} %select_select_fusion), channel_id=1, source_target_pairs={{0,8},{8,0},{16,24},{24,16},{1,9},{9,1},{17,25},{25,17},{2,10},{10... | collective-permute-start | bytes 270344 | tf_op jit(solution)/shard_map/ppermute | solution.py:28

commit v2 on v1

v2 whole, which is shorter than its diff:
```python
import functools

import jax
import jax.numpy as jnp
from jax import lax
from jax.experimental import pallas as pl
from jax.experimental.pallas import tpu as pltpu
from jax.sharding import PartitionSpec as P

ADAM_STEP = 20


ADAPTER_SCALE = 2.0
BETA_ONE = 0.9
BETA_TWO = 0.95
LEARN_RATE = 0.08
STABILITY_TERM = 1e-08

F32 = jnp.float32
BF16 = jnp.bfloat16
VMEM = pl.BlockSpec(memory_space=pltpu.VMEM)
HBM = pl.BlockSpec(memory_space=pltpu.HBM)
PARAMS = pltpu.CompilerParams(vmem_limit_bytes=16 * 1024 * 1024)


def adam_update(param, moment, second, grad):
    corr_one = 1.0 - BETA_ONE**ADAM_STEP
    corr_two = 1.0 - BETA_TWO**ADAM_STEP
    moment_new = BETA_ONE * moment + (1.0 - BETA_ONE) * grad
    second_new = BETA_TWO * second + (1.0 - BETA_TWO) * grad * grad
    param_new = param - LEARN_RATE * (moment_new / corr_one) / (
        jnp.sqrt(second_new / corr_two) + STABILITY_TERM
    )
    return (param_new, moment_new, second_new)


def swap(x, axis, n, k):
    return lax.ppermute(x, axis, [(i, i ^ k) for i in range(n)])


def held(x):
    return pltpu.with_memory_space_constraint(x, pltpu.VMEM)


def left(x):
    return pltpu.with_memory_space_constraint(x, pltpu.HBM)


def estimate(nbytes, flops=0):
    return pl.CostEstimate(flops=flops, bytes_accessed=nbytes, transcendentals=0)


def pack_kernel(n_dp, ranks, cols_a, grad_a, grad_b, *refs):
    outs, rows, sems = refs[: n_dp - 1], refs[n_dp - 1], refs[n_dp]
    me = lax.axis_index("dp")
    copies = []
    for k in range(1, n_dp):
        start = pl.multiple_of((me ^ k) * ranks, ranks)
        pair = (
            pltpu.make_async_copy(
                grad_a.at[0, 0, pl.ds(start, ranks), :],
                rows.at[k - 1, :, pl.ds(0, cols_a)],
                sems.at[k - 1, 0],
            ),
            pltpu.make_async_copy(
                grad_b.at[0, 0, pl.ds(start, ranks), :],
                rows.at[k - 1, :, pl.ds(cols_a, rows.shape[2] - cols_a)],
                sems.at[k - 1, 1],
            ),
        )
        for copy in pair:
            copy.start()
        copies.append(pair)
    for k, pair in enumerate(copies):
        for copy in pair:
            copy.wait()
        outs[k][...] = rows[k].astype(BF16)


def load_kernel(ranks, cols_a, *refs):
    grad_a, grad_b, fa, fb, ma, mb, sa, sb, weight = refs[:9]
    grad, factor, moment, second, panel, sems = refs[9:]
    me = lax.axis_index("dp")
    start = pl.multiple_of(me * ranks, ranks)
    left = pl.ds(0, cols_a)
    right = pl.ds(cols_a, grad.shape[1] - cols_a)
    pairs = [
        (grad_a.at[0, 0, pl.ds(start, ranks), :], grad.at[:, left]),
        (grad_b.at[0, 0, pl.ds(start, ranks), :], grad.at[:, right]),
        (fa.at[0], factor.at[:, left]),
        (fb.at[0], factor.at[:, right]),
        (ma.at[0], moment.at[:, left]),
        (mb.at[0], moment.at[:, right]),
        (sa.at[0], second.at[:, left]),
        (sb.at[0], second.at[:, right]),
        (weight.at[0], panel),
    ]
    copies = [pltpu.make_async_copy(a, b, sems.at[i]) for i, (a, b) in enumerate(pairs)]
    for copy in copies:
        copy.start()
    for copy in copies:
        copy.wait()


def send_kernel(*refs):
    grad, factor, moment, second = refs[:4]
    total = grad[...]
    for piece in refs[4:-1]:
        total = total + piece[...].astype(F32)
    refs[-1][...] = adam_update(factor[...], moment[...], second[...], total)[0].astype(BF16)


def state_kernel(n_got, cols_a, slot_of, *refs):
    grad, factor, moment, second = refs[:4]
    outs = refs[4 + n_got : -1]
    here = lax.axis_index("expert")
    wanted = jnp.int32(0)
    for expert in range(slot_of.shape[0]):
        wanted = jnp.where(slot_of[expert] == here, expert, wanted)
    refs[-1][...] = jnp.broadcast_to(wanted ^ here, refs[-1].shape)
    total = grad[...]
    for piece in refs[4 : 4 + n_got]:
        total = total + piece[...].astype(F32)
    for i, new in enumerate(adam_update(factor[...], moment[...], second[...], total)):
        outs[2 * i][0] = new[:, :cols_a]
        outs[2 * i + 1][0] = new[:, cols_a:]


def select_kernel(choice, *refs):
    wanted = choice[:1, :1]
    kept = refs[0][...]
    for k in range(1, len(refs) - 1):
        kept = jnp.where(wanted == k, refs[k][...], kept)
    refs[-1][...] = kept


def merge_kernel(k, n_parts, rows, *refs):
    panel, rows_a, rows_b = refs[0], refs[1], refs[2]
    out, flipped, tile, sems = refs[-4:]
    cols = rows_a.shape[1]
    total = panel.shape[0]
    at = (lax.axis_index("tensor") ^ k) * cols
    columns = pl.ds(pl.multiple_of(at, cols), cols)
    flipped[...] = (rows_b[...].astype(F32) * ADAPTER_SCALE).T.astype(BF16)
    copies = []
    for step in range(total // rows):
        here = pl.ds(step * rows, rows)
        increment = jnp.dot(flipped[here, :], rows_a[...], preferred_element_type=F32)
        tile[here, :] = (panel[here, columns].astype(F32) + increment).astype(BF16)
        copy = pltpu.make_async_copy(tile.at[here, :], out.at[0, here, columns], sems.at[step])
        copy.start()
        copies.append(copy)
    for copy in copies:
        copy.wait()


def per_device(
    n_dp,
    n_expert,
    n_tensor,
    weight,
    factor_a,
    factor_b,
    moment_a,
    second_a,
    first_moment_factor_b,
    second_b,
    grad_a,
    grad_b,
    slot_of,
):
    ranks, cols_a = factor_a.shape[1:]
    cols_b = factor_b.shape[2]
    cols = cols_a + cols_b

    pieces = pl.pallas_call(
        functools.partial(pack_kernel, n_dp, ranks, cols_a),
        in_specs=[HBM, HBM],
        out_specs=[VMEM] * (n_dp - 1),
        out_shape=[pltpu.VMEM((ranks, cols), BF16)] * (n_dp - 1),
        scratch_shapes=[
            pltpu.VMEM((n_dp - 1, ranks, cols), F32),
            pltpu.SemaphoreType.DMA((n_dp - 1, 2)),
        ],
        compiler_params=PARAMS,
        name="pack",
    )(left(grad_a), left(grad_b))
    got = [held(swap(piece, "dp", n_dp, k)) for k, piece in enumerate(pieces, 1)]

    panel_shape = weight.shape[1:]
    *state, panel = pl.pallas_call(
        functools.partial(load_kernel, ranks, cols_a),
        in_specs=[HBM] * 9,
        out_specs=[VMEM] * 5,
        out_shape=[pltpu.VMEM((ranks, cols), F32)] * 4 + [pltpu.VMEM(panel_shape, BF16)],
        scratch_shapes=[pltpu.SemaphoreType.DMA((9,))],
        compiler_params=PARAMS,
        cost_estimate=estimate(weight.size * 2 + 4 * ranks * cols * 4),
        name="load",
    )(
        *map(
            left,
            (
                grad_a,
                grad_b,
                factor_a,
                factor_b,
                moment_a,
                first_moment_factor_b,
                second_a,
                second_b,
                weight,
            ),
        )
    )
    state = [held(x) for x in state]
    panel = held(panel)

    send = pl.pallas_call(
        send_kernel,
        in_specs=[VMEM] * (3 + n_dp),
        out_specs=VMEM,
        out_shape=pltpu.VMEM((ranks, cols), BF16),
        compiler_params=PARAMS,
        name="send",
    )(*state, *got)

    others = [held(swap(send, "expert", n_expert, k)) for k in range(1, n_expert)]
    *new, choice = pl.pallas_call(
        functools.partial(state_kernel, n_dp - 1, cols_a),
        in_specs=[pl.BlockSpec(memory_space=pltpu.SMEM)] + [VMEM] * (3 + n_dp),
        out_specs=[VMEM] * 7,
        out_shape=[
            jax.ShapeDtypeStruct(factor_a.shape, F32),
            jax.ShapeDtypeStruct(factor_b.shape, F32),
        ]
        * 3
        + [pltpu.VMEM((8, 128), jnp.int32)],
        compiler_params=PARAMS,
        cost_estimate=estimate(3 * ranks * cols * 4),
        name="state",
    )(slot_of, *state, *got)
    new_a, new_b, new_moment_a, new_moment_b, new_second_a, new_second_b = new
    mine = pl.pallas_call(
        select_kernel,
        in_specs=[VMEM] * (n_expert + 1),
        out_specs=VMEM,
        out_shape=pltpu.VMEM((ranks, cols), BF16),
        compiler_params=PARAMS,
        name="select",
    )(held(choice), held(send), *others)

    parts = [mine] + [swap(mine, "dp", n_dp, k) for k in range(1, n_dp)]
    rows_a = jnp.concatenate([p[:, :cols_a] for p in parts], axis=0)
    rows_b = held(jnp.concatenate([p[:, cols_a:] for p in parts], axis=0))
    merged = None
    step_rows = 128
    for k in range(n_tensor):
        block = held(rows_a if k == 0 else swap(rows_a, "tensor", n_tensor, k))
        operands = [panel, block, rows_b] + ([] if merged is None else [merged])
        merged = pl.pallas_call(
            functools.partial(merge_kernel, k, n_dp, step_rows),
            in_specs=[VMEM] * 3 + [HBM] * (len(operands) - 3),
            out_specs=HBM,
            out_shape=jax.ShapeDtypeStruct(weight.shape, BF16),
            scratch_shapes=[
                pltpu.VMEM((cols_b, ranks * n_dp), BF16),
                pltpu.VMEM((panel_shape[0], cols_a), BF16),
                pltpu.SemaphoreType.DMA((panel_shape[0] // step_rows,)),
            ],
            input_output_aliases={} if merged is None else {3: 0},
            compiler_params=PARAMS,
            cost_estimate=estimate(
                panel_shape[0] * cols_a * 2, 2 * panel_shape[0] * cols_a * ranks * n_dp
            ),
            name=f"merge{k}",
        )(*operands)
    return (merged, new_a, new_b, new_moment_a, new_second_a, new_moment_b, new_second_b)


def solution(mesh):
    sizes = dict(mesh.shape)

    def body(*args):
        return per_device(sizes["dp"], sizes["expert"], sizes["tensor"], *args)

    state = P("expert", "dp", "tensor")
    grad = P("dp", "expert", None, "tensor")
    weight = P("expert", "tensor", None)
    in_specs = (weight,) + (state,) * 6 + (grad,) * 2 + (P(),)
    out_specs = (weight,) + (state,) * 6
    return jax.shard_map(body, mesh=mesh, in_specs=in_specs, out_specs=out_specs, check_vma=False)
```

time: 43.2 us -> 33.5 us (0.78); the launches traced: 42.6 us -> 33.4 us
  Pallas kernels: 0 us -> 10.2 us
  matrix products: 7.32 us -> 0 us
  blocking collectives: 6.43 us -> 0 us
  other arithmetic: 4.85 us -> 0.03 us
  local copies, waits for them, and re-layouts: 1.96 us -> 0.04 us
  starting transfers between devices: 9.88 us -> 11.8 us
  between operations: 1.38 us -> 0.73 us
    pallas_call x0 -> x7, Pallas kernels: none -> 10.2 us  [the longest x2 4.12 us: per_device(): pl.pallas_call(functools.partial(merge_kernel, k, n_dp, step_rows), in_sp...]
    dot_general x1 -> x0, matrix products: 7.32 us -> none  [per_device(): jnp.einsum('rf,rc->fc', rows_b, full_a, preferred_element_type=jnp.float32)]
    all_gather x1 -> x0, blocking collectives: 6.43 us -> none  [per_device(): full_a = lax.all_gather(rows_a, 'tensor', axis=1, tiled=True)]
    squeeze x2 -> x0, other arithmetic: 3.45 us -> none  [per_device(): send = jnp.concatenate([new_a[0], new_b[0]], axis=1).astype(jnp.bfloat16)]
    ppermute x9 -> x10, starting transfers between devices: 9.88 us -> 11.8 us  [swap(): return lax.ppermute(x, axis, [(i, i ^ k) for i in range(n)])]
    dynamic_slice x2 -> x0, local copies, waits for them, and re-layouts: 1.93 us -> none  [the longest x1 1.06 us: rows_of(): lax.dynamic_slice_in_dim(grad_a[0, 0], start, ranks, 0)]
    reduce_sum x1 -> x0, other arithmetic: 1.29 us -> none  [per_device(): wanted = jnp.sum(jnp.where(slot_of == here, experts, 0)) ^ here]
    ppermute x9 -> x10, waiting for transfers between devices: 10.8 us -> 10.6 us  [swap(): return lax.ppermute(x, axis, [(i, i ^ k) for i in range(n)])]
  transfers between devices with their start and end apart: 9 -> 10, of which waited for: 7 -> 6; matrix products, arithmetic and copies ran while one was open for 3% -> 0% of each run, Pallas kernels for 0% -> 20%
where the time goes in v2:
time: 33.5 us; the launch traced here: 33.4 us
  starting transfers between devices  11.8 us (35%)
  waiting for transfers between devices  10.6 us (32%)
  Pallas kernels  10.2 us (30%)
  between operations  0.73 us (2%)
    ppermute x10, starting transfers between devices, swap(): return lax.ppermute(x, axis, [(i, i ^ k) for i in range(n)])  11.8 us
    ppermute x10, waiting for transfers between devices, swap(): return lax.ppermute(x, axis, [(i, i ^ k) for i in range(n)])  10.6 us
    pallas_call x2, Pallas kernels, per_device(): pl.pallas_call(functools.partial(merge_kernel, k, n_dp, step_rows), in_sp...  4.12 us
    pallas_call x1, Pallas kernels, per_device(): pl.pallas_call(functools.partial(load_kernel, ranks, cols_a), in_specs=[H...  3.22 us
    pallas_call x1, Pallas kernels, per_device(): pl.pallas_call(functools.partial(state_kernel, n_dp - 1, cols_a), in_spec...  1.44 us
    pallas_call x1, Pallas kernels, per_device(): pl.pallas_call(functools.partial(pack_kernel, n_dp, ranks, cols_a), in_sp...  1.16 us
  transfers between devices with their start and end apart: 10, of which 6 were waited for; matrix products, arithmetic and copies ran while one was open for 0% of the time, Pallas kernels for 20%

profile of v2, /device:TPU:1, one launch (start us, length us, event | category | flops | bytes accessed | tf_op | source)
XLA Modules:
  0.0 33.4 jit_solution(8914661774090522014)
XLA Ops:
  0.6 0.0 copy-start
  0.6 1.2 %pack.1 = (bf16[16,2816]{1,0:T(8,128)(2,1)S(1)}, bf16[16,2816]{1,0:T(8,128)(2,1)S(1)}, bf16[16,2816]{1,0:T(8,128)(2,1)S(1)}) custom-call(f32[1,1,64,2048]{3,2,1,0:T(8,128)} %grad_a.1, f32[1,1,64,768]{3,2,1,0:T(8,128)} %grad_b.1), custom_call_target="tpu_custom_call" | custom-call | tf_op jit(solution)/shard_map/pack/pallas_call | solution.py:176
  1.8 2.1 %collective-permute-start = (bf16[16,2816]{1,0:T(8,128)(2,1)S(1)}, bf16[16,2816]{1,0:T(8,128)(2,1)S(1)}, u32[]{:S(2)}, u32[]{:S(2)}) collective-permute-start(bf16[16,2816]{1,0:T(8,128)(2,1)S(1)} %get-tuple-element.27), channel_id=1, source_target_pairs={{0,8},{8,0},{16,24},{24,16},{1,9},{9,1},{17,25},{25,17},{2,10},{10... | collective-permute-start | bytes 270344 | tf_op jit(solution)/shard_map/ppermute | solution.py:38
  3.9 1.2 %collective-permute-start.1 = (bf16[16,2816]{1,0:T(8,128)(2,1)S(1)}, bf16[16,2816]{1,0:T(8,128)(2,1)S(1)}, u32[]{:S(2)}, u32[]{:S(2)}) collective-permute-start(bf16[16,2816]{1,0:T(8,128)(2,1)S(1)} %get-tuple-element.28), channel_id=1, source_target_pairs={{0,16},{8,24},{16,0},{24,8},{1,17},{9,25},{17,1},{25,9},{2,18},{10... | collective-permute-start | bytes 270344 | tf_op jit(solution)/shard_map/ppermute | solution.py:38
  5.2 0.0 collective-permute-start.2
  5.2 3.2 %load.1 = (f32[16,2816]{1,0:T(8,128)S(1)}, f32[16,2816]{1,0:T(8,128)S(1)}, f32[16,2816]{1,0:T(8,128)S(1)}, f32[16,2816]{1,0:T(8,128)S(1)}, bf16[768,4096]{1,0:T(8,128)(2,1)S(1)}) custom-call(f32[1,1,64,2048]{3,2,1,0:T(8,128)} %grad_a.1, f32[1,1,64,768]{3,2,1,0:T(8,128)} %grad_b.1, f32[1,16,2048]{2,1,0:T(8,128)} %refs_2_.1, f32[1,16,768]{2,1,0:T(8,128)} %refs_3_.1, ...), custom_call_target="tpu_custom_call" | custom-call | bytes 7012352 | tf_op jit(solution)/shard_map/load/pallas_call | solution.py:191
  8.4 0.0 collective-permute-done.refs_4_
  8.4 0.0 collective-permute-done.1.refs_5_
  8.4 1.1 %collective-permute-done.2.refs_6_ = bf16[16,2816]{1,0:T(8,128)(2,1)S(1)} collective-permute-done((bf16[16,2816]{1,0:T(8,128)(2,1)S(1)}, bf16[16,2816]{1,0:T(8,128)(2,1)S(1)}, u32[]{:S(2)}, u32[]{:S(2)}) %collective-permute-start.2) | collective-permute-done | bytes 90144 | tf_op jit(solution)/shard_map/ppermute | solution.py:38
  9.5 0.2 send.1.refs_0_
  9.7 3.4 %collective-permute-start.5 = (bf16[16,2816]{1,0:T(8,128)(2,1)S(1)}, bf16[16,2816]{1,0:T(8,128)(2,1)S(1)}, u32[]{:S(2)}, u32[]{:S(2)}) collective-permute-start(bf16[16,2816]{1,0:T(8,128)(2,1)S(1)} %send.1.refs_0_), channel_id=1, source_target_pairs={{0,6},{2,4},{4,2},{6,0},{1,7},{3,5},{5,3},{7,1},{8,14},{10,12},{12... | collective-permute-start | bytes 270344 | tf_op jit(solution)/shard_map/ppermute | solution.py:38
  13.1 0.0 collective-permute-start.4
  13.1 0.4 %collective-permute-start.3 = (bf16[16,2816]{1,0:T(8,128)(2,1)S(1)}, bf16[16,2816]{1,0:T(8,128)(2,1)S(1)}, u32[]{:S(2)}, u32[]{:S(2)}) collective-permute-start(bf16[16,2816]{1,0:T(8,128)(2,1)S(1)} %send.1.refs_0_), channel_id=1, source_target_pairs={{0,2},{2,0},{4,6},{6,4},{1,3},{3,1},{5,7},{7,5},{8,10},{10,8},{12,... | collective-permute-start | bytes 270344 | tf_op jit(solution)/shard_map/ppermute | solution.py:38
  13.5 0.0 copy-done
  13.5 1.4 %state.1 = (f32[1,16,2048]{2,1,0:T(8,128)}, f32[1,16,768]{2,1,0:T(8,128)}, f32[1,16,2048]{2,1,0:T(8,128)}, f32[1,16,768]{2,1,0:T(8,128)}, f32[1,16,2048]{2,1,0:T...) custom-call(s32[4]{0:T(128)S(1)} %copy-done, f32[16,2816]{1,0:T(8,128)S(1)} %get-tuple-element.23.refs_0_, ...), custom_call_target="tpu_custom_call" | custom-call | bytes 540672 | tf_op jit(solution)/shard_map/state/pallas_call | solution.py:229
  14.9 0.2 collective-permute-done.5.refs_3_
  15.1 5.4 %collective-permute-done.4.refs_2_ = bf16[16,2816]{1,0:T(8,128)(2,1)S(1)} collective-permute-done((bf16[16,2816]{1,0:T(8,128)(2,1)S(1)}, bf16[16,2816]{1,0:T(8,128)(2,1)S(1)}, u32[]{:S(2)}, u32[]{:S(2)}) %collective-permute-start.4) | collective-permute-done | bytes 90144 | tf_op jit(solution)/shard_map/ppermute | solution.py:38
  20.6 0.0 collective-permute-done.3.refs_1_
  20.6 0.1 select.1
  20.6 1.3 %collective-permute-start.8 = (bf16[16,2816]{1,0:T(8,128)(2,1)S(1)}, bf16[16,2816]{1,0:T(8,128)(2,1)S(1)}, u32[]{:S(2)}, u32[]{:S(2)}) collective-permute-start(bf16[16,2816]{1,0:T(8,128)(2,1)S(1)} %select.1), channel_id=1, source_target_pairs={{0,24},{8,16},{16,8},{24,0},{1,25},{9,17},{17,9},{25,1},{2,26},{10... | collective-permute-start | bytes 270344 | tf_op jit(solution)/shard_map/ppermute | solution.py:38
  21.9 0.8 %collective-permute-start.7 = (bf16[16,2816]{1,0:T(8,128)(2,1)S(1)}, bf16[16,2816]{1,0:T(8,128)(2,1)S(1)}, u32[]{:S(2)}, u32[]{:S(2)}) collective-permute-start(bf16[16,2816]{1,0:T(8,128)(2,1)S(1)} %select.1), channel_id=1, source_target_pairs={{0,16},{8,24},{16,0},{24,8},{1,17},{9,25},{17,1},{25,9},{2,18},{10... | collective-permute-start | bytes 270344 | tf_op jit(solution)/shard_map/ppermute | solution.py:38
  22.7 0.7 %collective-permute-start.6 = (bf16[16,2816]{1,0:T(8,128)(2,1)S(1)}, bf16[16,2816]{1,0:T(8,128)(2,1)S(1)}, u32[]{:S(2)}, u32[]{:S(2)}) collective-permute-start(bf16[16,2816]{1,0:T(8,128)(2,1)S(1)} %select.1), channel_id=1, source_target_pairs={{0,8},{8,0},{16,24},{24,16},{1,9},{9,1},{17,25},{25,17},{2,10},{10... | collective-permute-start | bytes 270344 | tf_op jit(solution)/shard_map/ppermute | solution.py:38
  23.4 1.7 %collective-permute-done.8 = bf16[16,2816]{1,0:T(8,128)(2,1)S(1)} collective-permute-done((bf16[16,2816]{1,0:T(8,128)(2,1)S(1)}, bf16[16,2816]{1,0:T(8,128)(2,1)S(1)}, u32[]{:S(2)}, u32[]{:S(2)}) %collective-permute-start.8) | collective-permute-done | bytes 90144 | tf_op jit(solution)/shard_map/ppermute | solution.py:38
  25.0 1.3 %collective-permute-done.7 = bf16[16,2816]{1,0:T(8,128)(2,1)S(1)} collective-permute-done((bf16[16,2816]{1,0:T(8,128)(2,1)S(1)}, bf16[16,2816]{1,0:T(8,128)(2,1)S(1)}, u32[]{:S(2)}, u32[]{:S(2)}) %collective-permute-start.7) | collective-permute-done | bytes 90144 | tf_op jit(solution)/shard_map/ppermute | solution.py:38
  26.4 0.8 %collective-permute-done.6 = bf16[16,2816]{1,0:T(8,128)(2,1)S(1)} collective-permute-done((bf16[16,2816]{1,0:T(8,128)(2,1)S(1)}, bf16[16,2816]{1,0:T(8,128)(2,1)S(1)}, u32[]{:S(2)}, u32[]{:S(2)}) %collective-permute-start.6) | collective-permute-done | bytes 90144 | tf_op jit(solution)/shard_map/ppermute | solution.py:38
  27.2 2.0 %collective-permute-start.9 = (bf16[64,2048]{1,0:T(8,128)(2,1)S(1)}, bf16[64,2048]{1,0:T(8,128)(2,1)S(1)}, u32[]{:S(2)}, u32[]{:S(2)}) collective-permute-start(bf16[64,2048]{1,0:T(8,128)(2,1)S(1)} %pad_maximum_fusion.refs_1_), channel_id=1, source_target_pairs={{0,1},{1,0},{2,3},{3,2},{4,5},{5,4},{6,7},{7,6},{8,9},{9,8},{10,11... | collective-permute-start | bytes 786440 | tf_op jit(solution)/shard_map/ppermute | solution.py:38
  29.2 2.1 %merge0.1.refs_3_ = bf16[1,768,4096]{2,1,0:T(8,128)(2,1)} custom-call(bf16[768,4096]{1,0:T(8,128)(2,1)S(1)} %get-tuple-element.22.refs_0_, bf16[64,2048]{1,0:T(8,128)(2,1)S(1)} %pad_maximum_fusion.refs_1_, bf16[64,768]{1,0:T(8,128)(2,1)S(1)} %pad_maximum_fusion.1.refs_2_), custom_call_target="tpu_custom_call" | custom-call | flops 201326592 | bytes 3145728 | tf_op jit(solution)/shard_map/merge0/pallas_call | solution.py:261
  31.3 0.0 collective-permute-done.9.refs_1_
  31.3 2.1 %merge1.1 = bf16[1,768,4096]{2,1,0:T(8,128)(2,1)} custom-call(bf16[768,4096]{1,0:T(8,128)(2,1)S(1)} %get-tuple-element.22.refs_0_, bf16[64,2048]{1,0:T(8,128)(2,1)S(1)} %collective-permute-done.9.refs_1_, bf16[64,768]{1,0:T(8,128)(2,1)S(1)} %pad_maximum_fusion.1.refs_2_, bf16[1,768,4096]{2,1,0:T(8,128)(2,1)} %merge0.1.refs_3_), custom_call_target="tpu_custom_call", output_to_operand_aliasing={{}: (3, {})} | custom-call | flops 201326592 | bytes 3145728 | tf_op jit(solution)/shard_map/merge1/pallas_call | solution.py:261
  (10 shorter events, 0.1 us)
Async XLA Ops:
  0.6 12.8 %copy-start = (s32[4]{0:T(128)S(1)}, s32[4]{0:T(128)}, u32[]{:S(2)}) copy-start(s32[4]{0:T(128)} %slot_of.1) | copy-start | bytes 52
  1.8 6.6 %collective-permute-start = (bf16[16,2816]{1,0:T(8,128)(2,1)S(1)}, bf16[16,2816]{1,0:T(8,128)(2,1)S(1)}, u32[]{:S(2)}, u32[]{:S(2)}) collective-permute-start(bf16[16,2816]{1,0:T(8,128)(2,1)S(1)} %get-tuple-element.27), channel_id=1, source_target_pairs={{0,8},{8,0},{16,24},{24,16},{1,9},{9,1},{17,25},{25,17},{2,10},{10... | collective-permute-start | bytes 270344 | tf_op jit(solution)/shard_map/ppermute | solution.py:38
  3.9 4.5 %collective-permute-start.1 = (bf16[16,2816]{1,0:T(8,128)(2,1)S(1)}, bf16[16,2816]{1,0:T(8,128)(2,1)S(1)}, u32[]{:S(2)}, u32[]{:S(2)}) collective-permute-start(bf16[16,2816]{1,0:T(8,128)(2,1)S(1)} %get-tuple-element.28), channel_id=1, source_target_pairs={{0,16},{8,24},{16,0},{24,8},{1,17},{9,25},{17,1},{25,9},{2,18},{10... | collective-permute-start | bytes 270344 | tf_op jit(solution)/shard_map/ppermute | solution.py:38
  5.2 4.4 %collective-permute-start.2 = (bf16[16,2816]{1,0:T(8,128)(2,1)S(1)}, bf16[16,2816]{1,0:T(8,128)(2,1)S(1)}, u32[]{:S(2)}, u32[]{:S(2)}) collective-permute-start(bf16[16,2816]{1,0:T(8,128)(2,1)S(1)} %get-tuple-element.29), channel_id=1, source_target_pairs={{0,24},{8,16},{16,8},{24,0},{1,25},{9,17},{17,9},{25,1},{2,26},{10... | collective-permute-start | bytes 270344 | tf_op jit(solution)/shard_map/ppermute | solution.py:38
  9.7 5.4 %collective-permute-start.5 = (bf16[16,2816]{1,0:T(8,128)(2,1)S(1)}, bf16[16,2816]{1,0:T(8,128)(2,1)S(1)}, u32[]{:S(2)}, u32[]{:S(2)}) collective-permute-start(bf16[16,2816]{1,0:T(8,128)(2,1)S(1)} %send.1.refs_0_), channel_id=1, source_target_pairs={{0,6},{2,4},{4,2},{6,0},{1,7},{3,5},{5,3},{7,1},{8,14},{10,12},{12... | collective-permute-start | bytes 270344 | tf_op jit(solution)/shard_map/ppermute | solution.py:38
  13.1 7.5 %collective-permute-start.4 = (bf16[16,2816]{1,0:T(8,128)(2,1)S(1)}, bf16[16,2816]{1,0:T(8,128)(2,1)S(1)}, u32[]{:S(2)}, u32[]{:S(2)}) collective-permute-start(bf16[16,2816]{1,0:T(8,128)(2,1)S(1)} %send.1.refs_0_), channel_id=1, source_target_pairs={{0,4},{2,6},{4,0},{6,2},{1,5},{3,7},{5,1},{7,3},{8,12},{10,14},{12... | collective-permute-start | bytes 270344 | tf_op jit(solution)/shard_map/ppermute | solution.py:38
  13.1 7.5 %collective-permute-start.3 = (bf16[16,2816]{1,0:T(8,128)(2,1)S(1)}, bf16[16,2816]{1,0:T(8,128)(2,1)S(1)}, u32[]{:S(2)}, u32[]{:S(2)}) collective-permute-start(bf16[16,2816]{1,0:T(8,128)(2,1)S(1)} %send.1.refs_0_), channel_id=1, source_target_pairs={{0,2},{2,0},{4,6},{6,4},{1,3},{3,1},{5,7},{7,5},{8,10},{10,8},{12,... | collective-permute-start | bytes 270344 | tf_op jit(solution)/shard_map/ppermute | solution.py:38
  20.6 4.4 %collective-permute-start.8 = (bf16[16,2816]{1,0:T(8,128)(2,1)S(1)}, bf16[16,2816]{1,0:T(8,128)(2,1)S(1)}, u32[]{:S(2)}, u32[]{:S(2)}) collective-permute-start(bf16[16,2816]{1,0:T(8,128)(2,1)S(1)} %select.1), channel_id=1, source_target_pairs={{0,24},{8,16},{16,8},{24,0},{1,25},{9,17},{17,9},{25,1},{2,26},{10... | collective-permute-start | bytes 270344 | tf_op jit(solution)/shard_map/ppermute | solution.py:38
  21.9 4.4 %collective-permute-start.7 = (bf16[16,2816]{1,0:T(8,128)(2,1)S(1)}, bf16[16,2816]{1,0:T(8,128)(2,1)S(1)}, u32[]{:S(2)}, u32[]{:S(2)}) collective-permute-start(bf16[16,2816]{1,0:T(8,128)(2,1)S(1)} %select.1), channel_id=1, source_target_pairs={{0,16},{8,24},{16,0},{24,8},{1,17},{9,25},{17,1},{25,9},{2,18},{10... | collective-permute-start | bytes 270344 | tf_op jit(solution)/shard_map/ppermute | solution.py:38
  22.7 4.4 %collective-permute-start.6 = (bf16[16,2816]{1,0:T(8,128)(2,1)S(1)}, bf16[16,2816]{1,0:T(8,128)(2,1)S(1)}, u32[]{:S(2)}, u32[]{:S(2)}) collective-permute-start(bf16[16,2816]{1,0:T(8,128)(2,1)S(1)} %select.1), channel_id=1, source_target_pairs={{0,8},{8,0},{16,24},{24,16},{1,9},{9,1},{17,25},{25,17},{2,10},{10... | collective-permute-start | bytes 270344 | tf_op jit(solution)/shard_map/ppermute | solution.py:38
  27.2 4.1 %collective-permute-start.9 = (bf16[64,2048]{1,0:T(8,128)(2,1)S(1)}, bf16[64,2048]{1,0:T(8,128)(2,1)S(1)}, u32[]{:S(2)}, u32[]{:S(2)}) collective-permute-start(bf16[64,2048]{1,0:T(8,128)(2,1)S(1)} %pad_maximum_fusion.refs_1_), channel_id=1, source_target_pairs={{0,1},{1,0},{2,3},{3,2},{4,5},{5,4},{6,7},{7,6},{8,9},{9,8},{10,11... | collective-permute-start | bytes 786440 | tf_op jit(solution)/shard_map/ppermute | solution.py:38

commit v3 on v2

v3 whole, which is shorter than its diff:
```python
import functools
import itertools

import jax
import jax.numpy as jnp
from jax import lax
from jax.experimental import pallas as pl
from jax.experimental.pallas import tpu as pltpu
from jax.sharding import PartitionSpec as P

ADAM_STEP = 20


ADAPTER_SCALE = 2.0
BETA_ONE = 0.9
BETA_TWO = 0.95
LEARN_RATE = 0.08
STABILITY_TERM = 1e-08

MOST_SWITCHED = 4

F32 = jnp.float32
BF16 = jnp.bfloat16
VMEM = pl.BlockSpec(memory_space=pltpu.VMEM)
SMEM = pl.BlockSpec(memory_space=pltpu.SMEM)
HBM = pl.BlockSpec(memory_space=pltpu.HBM)
PARAMS = pltpu.CompilerParams(vmem_limit_bytes=16 * 1024 * 1024)


def adam_update(param, moment, second, grad):
    corr_one = 1.0 - BETA_ONE**ADAM_STEP
    corr_two = 1.0 - BETA_TWO**ADAM_STEP
    moment_new = BETA_ONE * moment + (1.0 - BETA_ONE) * grad
    second_new = BETA_TWO * second + (1.0 - BETA_TWO) * grad * grad
    param_new = param - LEARN_RATE * (moment_new / corr_one) / (
        jnp.sqrt(second_new / corr_two) + STABILITY_TERM
    )
    return (param_new, moment_new, second_new)


def swap(x, axis, n, k):
    return lax.ppermute(x, axis, [(i, i ^ k) for i in range(n)])


def held(x):
    return pltpu.with_memory_space_constraint(x, pltpu.VMEM)


def left(x):
    return pltpu.with_memory_space_constraint(x, pltpu.HBM)


def estimate(nbytes, flops=0):
    return pl.CostEstimate(flops=flops, bytes_accessed=nbytes, transcendentals=0)


def pack_kernel(n_dp, ranks, cols_a, grad_a, grad_b, *refs):
    outs, rows, sems = refs[: n_dp - 1], refs[n_dp - 1], refs[n_dp]
    me = lax.axis_index("dp")
    copies = []
    for k in range(1, n_dp):
        start = pl.multiple_of((me ^ k) * ranks, ranks)
        pair = (
            pltpu.make_async_copy(
                grad_a.at[0, 0, pl.ds(start, ranks), :],
                rows.at[k - 1, :, pl.ds(0, cols_a)],
                sems.at[k - 1, 0],
            ),
            pltpu.make_async_copy(
                grad_b.at[0, 0, pl.ds(start, ranks), :],
                rows.at[k - 1, :, pl.ds(cols_a, rows.shape[2] - cols_a)],
                sems.at[k - 1, 1],
            ),
        )
        for copy in pair:
            copy.start()
        copies.append(pair)
    for k, pair in enumerate(copies):
        for copy in pair:
            copy.wait()
        outs[k][...] = rows[k].astype(BF16)


def load_kernel(ranks, cols_a, slot_of, *refs):
    grad_a, grad_b, fa, fb, ma, mb, sa, sb = refs[:8]
    grad, factor, moment, second, order, sems = refs[8:]
    me = lax.axis_index("dp")
    start = pl.multiple_of(me * ranks, ranks)
    first = pl.ds(0, cols_a)
    last = pl.ds(cols_a, grad.shape[1] - cols_a)
    pairs = [
        (grad_a.at[0, 0, pl.ds(start, ranks), :], grad.at[:, first]),
        (grad_b.at[0, 0, pl.ds(start, ranks), :], grad.at[:, last]),
        (fa.at[0], factor.at[:, first]),
        (fb.at[0], factor.at[:, last]),
        (ma.at[0], moment.at[:, first]),
        (mb.at[0], moment.at[:, last]),
        (sa.at[0], second.at[:, first]),
        (sb.at[0], second.at[:, last]),
    ]
    copies = [pltpu.make_async_copy(a, b, sems.at[i]) for i, (a, b) in enumerate(pairs)]
    for copy in copies:
        copy.start()
    n = slot_of.shape[0]
    number = jnp.int32(0)
    for i in range(n - 1):
        smaller = jnp.int32(0)
        for j in range(i + 1, n):
            smaller += (slot_of[j] < slot_of[i]).astype(jnp.int32)
        number = number * (n - i) + smaller
    order[0] = number
    for copy in copies:
        copy.wait()


def panel_kernel(weight, panel, sem):
    copy = pltpu.make_async_copy(weight.at[0], panel, sem)
    copy.start()
    copy.wait()


def send_kernel(*refs):
    grad, factor, moment, second = refs[:4]
    total = grad[...]
    for piece in refs[4:-1]:
        total = total + piece[...].astype(F32)
    refs[-1][...] = adam_update(factor[...], moment[...], second[...], total)[0].astype(BF16)


def state_kernel(n_got, cols_a, *refs):
    grad, factor, moment, second = refs[:4]
    outs = refs[4 + n_got :]
    total = grad[...]
    for piece in refs[4 : 4 + n_got]:
        total = total + piece[...].astype(F32)
    for i, new in enumerate(adam_update(factor[...], moment[...], second[...], total)):
        outs[2 * i][0] = new[:, :cols_a]
        outs[2 * i + 1][0] = new[:, cols_a:]


def join_kernel(cols_a, *refs):
    parts = refs[:-4]
    rows_a, flipped = refs[-3:-1]
    ranks = parts[0].shape[0]
    for i, part in enumerate(parts):
        rows_a[pl.ds(i * ranks, ranks), :] = part[:, :cols_a]
    rows_b = jnp.concatenate([part[:, cols_a:].astype(F32) for part in parts], axis=0)
    flipped[...] = (rows_b * ADAPTER_SCALE).T.astype(BF16)


def merge_kernel(k, width, *refs):
    panel, rows_a, flipped = refs[:3]
    out, tiles, sems = refs[-3:]
    cols = rows_a.shape[1]
    base = (lax.axis_index("tensor") ^ k) * cols
    copies = []
    for step in range(cols // width):
        columns = pl.ds(pl.multiple_of(base + step * width, width), width)
        increment = jnp.dot(
            flipped[...], rows_a[:, step * width : (step + 1) * width], preferred_element_type=F32
        )
        tiles[step] = (panel[:, columns].astype(F32) + increment).astype(BF16)
        copy = pltpu.make_async_copy(tiles.at[step], out.at[0, :, columns], sems.at[step])
        copy.start()
        copies.append(copy)
    for copy in copies:
        copy.wait()


def per_device(
    n_dp,
    n_expert,
    n_tensor,
    weight,
    factor_a,
    factor_b,
    moment_a,
    second_a,
    first_moment_factor_b,
    second_b,
    grad_a,
    grad_b,
    slot_of,
):
    ranks, cols_a = factor_a.shape[1:]
    cols_b = factor_b.shape[2]
    cols = cols_a + cols_b

    pieces = pl.pallas_call(
        functools.partial(pack_kernel, n_dp, ranks, cols_a),
        in_specs=[HBM, HBM],
        out_specs=[VMEM] * (n_dp - 1),
        out_shape=[pltpu.VMEM((ranks, cols), BF16)] * (n_dp - 1),
        scratch_shapes=[
            pltpu.VMEM((n_dp - 1, ranks, cols), F32),
            pltpu.SemaphoreType.DMA((n_dp - 1, 2)),
        ],
        compiler_params=PARAMS,
        name="pack",
    )(left(grad_a), left(grad_b))
    got = [held(swap(piece, "dp", n_dp, k)) for k, piece in enumerate(pieces, 1)]

    *state, order = pl.pallas_call(
        functools.partial(load_kernel, ranks, cols_a),
        in_specs=[SMEM] + [HBM] * 8,
        out_specs=[VMEM] * 4 + [SMEM],
        out_shape=[pltpu.VMEM((ranks, cols), F32)] * 4 + [pltpu.SMEM((1,), jnp.int32)],
        scratch_shapes=[pltpu.SemaphoreType.DMA((8,))],
        compiler_params=PARAMS,
        cost_estimate=estimate(4 * ranks * cols * 4),
        name="load",
    )(
        slot_of,
        *map(
            left,
            (
                grad_a,
                grad_b,
                factor_a,
                factor_b,
                moment_a,
                first_moment_factor_b,
                second_a,
                second_b,
            ),
        ),
    )
    state = [held(x) for x in state]

    send = pl.pallas_call(
        send_kernel,
        in_specs=[VMEM] * (3 + n_dp),
        out_specs=VMEM,
        out_shape=pltpu.VMEM((ranks, cols), BF16),
        compiler_params=PARAMS,
        name="send",
    )(*state, *got)

    def move(slots):
        def branch(send, state, got):
            mine = lax.ppermute(send, "expert", list(enumerate(slots)))
            new = pl.pallas_call(
                functools.partial(state_kernel, n_dp - 1, cols_a),
                in_specs=[VMEM] * (3 + n_dp),
                out_specs=[VMEM] * 6,
                out_shape=[
                    jax.ShapeDtypeStruct(factor_a.shape, F32),
                    jax.ShapeDtypeStruct(factor_b.shape, F32),
                ]
                * 3,
                compiler_params=PARAMS,
                cost_estimate=estimate(3 * ranks * cols * 4),
                name="state",
            )(*map(held, state), *map(held, got))
            return mine, new

        return branch

    if n_expert <= MOST_SWITCHED:
        orders = list(itertools.permutations(range(n_expert)))
        mine, new = lax.switch(order[0], [move(slots) for slots in orders], send, state, got)
    else:
        mine, new = move(range(n_expert))(send, state, got)
        here = lax.axis_index("expert")
        experts = jnp.arange(n_expert, dtype=jnp.int32)
        wanted = jnp.sum(jnp.where(slot_of == here, experts, 0)) ^ here
        for k in range(1, n_expert):
            mine = jnp.where(wanted == k, swap(send, "expert", n_expert, k), mine)
    new_a, new_b, new_moment_a, new_moment_b, new_second_a, new_second_b = new

    parts = [mine] + [swap(mine, "dp", n_dp, k) for k in range(1, n_dp)]
    panel_shape = weight.shape[1:]
    panel = pl.pallas_call(
        panel_kernel,
        in_specs=[HBM],
        out_specs=VMEM,
        out_shape=pltpu.VMEM(panel_shape, BF16),
        scratch_shapes=[pltpu.SemaphoreType.DMA],
        compiler_params=PARAMS,
        cost_estimate=estimate(weight.size * 4),
        name="panel",
    )(left(weight))
    rows_a, flipped, panel = pl.pallas_call(
        functools.partial(join_kernel, cols_a),
        in_specs=[VMEM] * (n_dp + 1),
        out_specs=[VMEM] * 3,
        out_shape=[
            pltpu.VMEM((ranks * n_dp, cols_a), BF16),
            pltpu.VMEM((cols_b, ranks * n_dp), BF16),
            pltpu.VMEM(panel_shape, BF16),
        ],
        input_output_aliases={n_dp: 2},
        compiler_params=PARAMS,
        name="join",
    )(*map(held, parts), held(panel))

    merged = None
    width = 512
    for k in range(n_tensor):
        block = held(rows_a if k == 0 else swap(rows_a, "tensor", n_tensor, k))
        operands = [held(panel), block, held(flipped)] + ([] if merged is None else [merged])
        merged = pl.pallas_call(
            functools.partial(merge_kernel, k, width),
            in_specs=[VMEM] * 3 + [HBM] * (len(operands) - 3),
            out_specs=HBM,
            out_shape=jax.ShapeDtypeStruct(weight.shape, BF16),
            scratch_shapes=[
                pltpu.VMEM((cols_a // width, panel_shape[0], width), BF16),
                pltpu.SemaphoreType.DMA((cols_a // width,)),
            ],
            input_output_aliases={} if merged is None else {3: 0},
            compiler_params=PARAMS,
            cost_estimate=estimate(
                panel_shape[0] * cols_a * 2, 2 * panel_shape[0] * cols_a * ranks * n_dp
            ),
            name=f"merge{k}",
        )(*operands)
    return (merged, new_a, new_b, new_moment_a, new_second_a, new_moment_b, new_second_b)


def solution(mesh):
    sizes = dict(mesh.shape)

    def body(*args):
        return per_device(sizes["dp"], sizes["expert"], sizes["tensor"], *args)

    state = P("expert", "dp", "tensor")
    grad = P("dp", "expert", None, "tensor")
    weight = P("expert", "tensor", None)
    in_specs = (weight,) + (state,) * 6 + (grad,) * 2 + (P(),)
    out_specs = (weight,) + (state,) * 6
    return jax.shard_map(body, mesh=mesh, in_specs=in_specs, out_specs=out_specs, check_vma=False)
```

time: 33.5 us -> 32.2 us (0.961); the launches traced: 33.4 us -> 31.6 us
  waiting for transfers between devices: 10.6 us -> 2.64 us
  starting transfers between devices: 11.8 us -> 15.6 us
  Pallas kernels: 10.2 us -> 11.9 us
  local copies, waits for them, and re-layouts: 0.04 us -> 0.65 us
    ppermute x10 -> x7, waiting for transfers between devices: 10.6 us -> 2 us  [swap(): return lax.ppermute(x, axis, [(i, i ^ k) for i in range(n)])]
    ppermute x0 -> x1, starting transfers between devices: none -> 5.23 us  [branch(): mine = lax.ppermute(send, 'expert', list(enumerate(slots)))]
    pallas_call x5 -> x6, Pallas kernels: 8.84 us -> 10.6 us  [the longest x2 4.06 us: per_device(): pl.pallas_call(functools.partial(merge_kernel, k, width), in_specs=[VMEM]...]
    ppermute x10 -> x7, starting transfers between devices: 11.8 us -> 10.4 us  [swap(): return lax.ppermute(x, axis, [(i, i ^ k) for i in range(n)])]
    unnamed x2, local copies, waits for them, and re-layouts: 0.01 us -> 0.65 us
    ppermute x0 -> x1, waiting for transfers between devices: none -> 0.63 us  [branch(): mine = lax.ppermute(send, 'expert', list(enumerate(slots)))]
  transfers between devices with their start and end apart: 10 -> 8, of which waited for: 6 -> 3; matrix products, arithmetic and copies ran while one was open for 0% -> 0% of each run, Pallas kernels for 20% -> 24%
where the time goes in v3:
time: 32.2 us; the launch traced here: 31.6 us
  starting transfers between devices  15.6 us (48%)
  Pallas kernels  11.9 us (37%)
  waiting for transfers between devices  2.64 us (8%)
  between operations  0.72 us (2%)
  local copies, waits for them, and re-layouts  0.65 us (2%)
    ppermute x7, starting transfers between devices, swap(): return lax.ppermute(x, axis, [(i, i ^ k) for i in range(n)])  10.4 us
    ppermute x1, starting transfers between devices, branch(): mine = lax.ppermute(send, 'expert', list(enumerate(slots)))  5.23 us
    pallas_call x2, Pallas kernels, per_device(): pl.pallas_call(functools.partial(merge_kernel, k, width), in_specs=[VMEM]...  4.06 us
    pallas_call x1, Pallas kernels, per_device(): pl.pallas_call(panel_kernel, in_specs=[HBM], out_specs=VMEM, out_shape=pl...  2.79 us
    ppermute x7, waiting for transfers between devices, swap(): return lax.ppermute(x, axis, [(i, i ^ k) for i in range(n)])  2 us
    pallas_call x1, Pallas kernels, per_device(): pl.pallas_call(functools.partial(load_kernel, ranks, cols_a), in_specs=[S...  1.8 us
    pallas_call x1, Pallas kernels, per_device(): pl.pallas_call(functools.partial(pack_kernel, n_dp, ranks, cols_a), in_sp...  1.16 us
    pallas_call x1, Pallas kernels, per_device(): pl.pallas_call(functools.partial(join_kernel, cols_a), in_specs=[VMEM] *...  1.04 us
  transfers between devices with their start and end apart: 8, of which 3 were waited for; matrix products, arithmetic and copies ran while one was open for 0% of the time, Pallas kernels for 24%

profile of v3, /device:TPU:1, one launch (start us, length us, event | category | flops | bytes accessed | tf_op | source)
XLA Modules:
  0.0 31.6 jit_solution(10287999107450239847)
XLA Ops:
  0.6 1.2 %pack.1 = (bf16[16,2816]{1,0:T(8,128)(2,1)S(1)}, bf16[16,2816]{1,0:T(8,128)(2,1)S(1)}, bf16[16,2816]{1,0:T(8,128)(2,1)S(1)}) custom-call(f32[1,1,64,2048]{3,2,1,0:T(8,128)} %grad_a.1, f32[1,1,64,768]{3,2,1,0:T(8,128)} %grad_b.1), custom_call_target="tpu_custom_call" | custom-call | tf_op jit(solution)/shard_map/pack/pallas_call | solution.py:189
  1.8 2.1 %collective-permute-start.24 = (bf16[16,2816]{1,0:T(8,128)(2,1)S(1)}, bf16[16,2816]{1,0:T(8,128)(2,1)S(1)}, u32[]{:S(2)}, u32[]{:S(2)}) collective-permute-start(bf16[16,2816]{1,0:T(8,128)(2,1)S(1)} %get-tuple-element.750), channel_id=1, source_target_pairs={{0,8},{8,0},{16,24},{24,16},{1,9},{9,1},{17,25},{25,17},{2,10},{10... | collective-permute-start | bytes 270344 | tf_op jit(solution)/shard_map/ppermute | solution.py:42
  3.9 1.2 %collective-permute-start.25 = (bf16[16,2816]{1,0:T(8,128)(2,1)S(1)}, bf16[16,2816]{1,0:T(8,128)(2,1)S(1)}, u32[]{:S(2)}, u32[]{:S(2)}) collective-permute-start(bf16[16,2816]{1,0:T(8,128)(2,1)S(1)} %get-tuple-element.751), channel_id=1, source_target_pairs={{0,16},{8,24},{16,0},{24,8},{1,17},{9,25},{17,1},{25,9},{2,18},{10... | collective-permute-start | bytes 270344 | tf_op jit(solution)/shard_map/ppermute | solution.py:42
  5.1 0.0 collective-permute-start.26
  5.2 0.0 copy-start
  5.2 0.7 %copy-done = s32[4]{0:T(128)S(1)} copy-done((s32[4]{0:T(128)S(1)}, s32[4]{0:T(128)}, u32[]{:S(2)}) %copy-start) | copy-done | bytes 40
  5.8 1.8 %load.1 = (f32[16,2816]{1,0:T(8,128)S(1)}, f32[16,2816]{1,0:T(8,128)S(1)}, f32[16,2816]{1,0:T(8,128)S(1)}, f32[16,2816]{1,0:T(8,128)S(1)}, s32[1]{0:T(128)S(4)}) custom-call(s32[4]{0:T(128)S(1)} %copy-done, f32[1,1,64,2048]{3,2,1,0:T(8,128)} %grad_a.1, f32[1,1,64,768]{3,2,1,0:T(8,128)} %grad_b.1, f32[1,16,2048]{2,1,0:T(8,128)} %refs_2_.1, ...), custom_call_target="tpu_custom_call" | custom-call | bytes 720896 | tf_op jit(solution)/shard_map/load/pallas_call | solution.py:203
  7.6 0.0 collective-permute-done.24.refs_4_
  7.6 0.0 collective-permute-done.25.refs_5_
  7.7 1.9 %collective-permute-done.26.refs_6_ = bf16[16,2816]{1,0:T(8,128)(2,1)S(1)} collective-permute-done((bf16[16,2816]{1,0:T(8,128)(2,1)S(1)}, bf16[16,2816]{1,0:T(8,128)(2,1)S(1)}, u32[]{:S(2)}, u32[]{:S(2)}) %collective-permute-start.26) | collective-permute-done | bytes 90144 | tf_op jit(solution)/shard_map/ppermute | solution.py:42
  9.5 0.2 send.1
  9.7 6.8 %conditional.1 = (bf16[16,2816]{1,0:T(8,128)(2,1)}, f32[1,16,2048]{2,1,0:T(8,128)}, f32[1,16,768]{2,1,0:T(8,128)}, f32[1,16,2048]{2,1,0:T(8,128)}, f32[1,16,768]...) conditional(s32[]{:T(128)} %bitcast, ...), branch_computations={%region_0.0_spmd, %region_1.0_spmd, %region_2.0_spmd, %region_3.0_... | conditional | bytes 901216 | solution.py:261
  9.8 5.2 %collective-permute-start.19 = (bf16[16,2816]{1,0:T(8,128)(2,1)S(1)}, bf16[16,2816]{1,0:T(8,128)(2,1)}, u32[]{:S(2)}, u32[]{:S(2)}) collective-permute-start(bf16[16,2816]{1,0:T(8,128)(2,1)S(1)} %get-tuple-element.650), channel_id=1, source_target_pairs={{0,6},{2,0},{4,4},{6,2},{1,7},{3,1},{5,5},{7,3},{8,14},{10,8},{12,... | collective-permute-start | bytes 270344 | tf_op jit(solution)/shard_map/cond/branch_19_fun/ppermute | solution.py:241
  15.0 0.9 %state.43 = (f32[1,16,2048]{2,1,0:T(8,128)}, f32[1,16,768]{2,1,0:T(8,128)}, f32[1,16,2048]{2,1,0:T(8,128)}, f32[1,16,768]{2,1,0:T(8,128)}, f32[1,16,2048]{2,1,0:T(8,128)}, /*index=5*/f32[1,16,768]{2,1,0:T(8,128)}) custom-call(f32[16,2816]{1,0:T(8,128)S(1)} %get-tuple-element.651.refs_0_, f32[16,2816]{1,0:T(8,128)S(1)} %get-tuple-element.652.refs_1_, ...), custom_call_target="tpu_custom_call" | custom-call | bytes 540672 | tf_op jit(solution)/shard_map/cond/branch_19_fun/state/pallas_call | solution.py:242
  15.9 0.6 %collective-permute-done.19 = bf16[16,2816]{1,0:T(8,128)(2,1)} collective-permute-done((bf16[16,2816]{1,0:T(8,128)(2,1)S(1)}, bf16[16,2816]{1,0:T(8,128)(2,1)}, u32[]{:S(2)}, u32[]{:S(2)}) %collective-permute-start.19) | collective-permute-done | bytes 90144 | tf_op jit(solution)/shard_map/cond/branch_19_fun/ppermute | solution.py:241
  16.5 0.9 %collective-permute-start.29 = (bf16[16,2816]{1,0:T(8,128)(2,1)}, bf16[16,2816]{1,0:T(8,128)(2,1)S(1)}, u32[]{:S(2)}, u32[]{:S(2)}) collective-permute-start(bf16[16,2816]{1,0:T(8,128)(2,1)} %get-tuple-element.753.refs_0_), channel_id=1, source_target_pairs={{0,24},{8,16},{16,8},{24,0},{1,25},{9,17},{17,9},{25,1},{2,26},{10... | collective-permute-start | bytes 270344 | tf_op jit(solution)/shard_map/ppermute | solution.py:42
  17.4 1.1 %collective-permute-start.28 = (bf16[16,2816]{1,0:T(8,128)(2,1)}, bf16[16,2816]{1,0:T(8,128)(2,1)S(1)}, u32[]{:S(2)}, u32[]{:S(2)}) collective-permute-start(bf16[16,2816]{1,0:T(8,128)(2,1)} %get-tuple-element.753.refs_0_), channel_id=1, source_target_pairs={{0,16},{8,24},{16,0},{24,8},{1,17},{9,25},{17,1},{25,9},{2,18},{10... | collective-permute-start | bytes 270344 | tf_op jit(solution)/shard_map/ppermute | solution.py:42
  18.5 0.7 %collective-permute-start.27 = (bf16[16,2816]{1,0:T(8,128)(2,1)}, bf16[16,2816]{1,0:T(8,128)(2,1)S(1)}, u32[]{:S(2)}, u32[]{:S(2)}) collective-permute-start(bf16[16,2816]{1,0:T(8,128)(2,1)} %get-tuple-element.753.refs_0_), channel_id=1, source_target_pairs={{0,8},{8,0},{16,24},{24,16},{1,9},{9,1},{17,25},{25,17},{2,10},{10... | collective-permute-start | bytes 270344 | tf_op jit(solution)/shard_map/ppermute | solution.py:42
  19.2 2.8 %panel.1.refs_4_ = bf16[768,4096]{1,0:T(8,128)(2,1)S(1)} custom-call(bf16[1,768,4096]{2,1,0:T(8,128)(2,1)} %weight.1), custom_call_target="tpu_custom_call" | custom-call | bytes 12582912 | tf_op jit(solution)/shard_map/panel/pallas_call | solution.py:273
  22.0 0.0 collective-permute-done.29.refs_3_
  22.0 0.0 collective-permute-done.28.refs_2_
  22.0 0.1 collective-permute-done.27.refs_1_
  22.1 1.0 %join.1 = (bf16[64,2048]{1,0:T(8,128)(2,1)S(1)}, bf16[768,64]{1,0:T(8,128)(2,1)S(1)}, bf16[768,4096]{1,0:T(8,128)(2,1)S(1)}) custom-call(bf16[16,2816]{1,0:T(8,128)(2,1)} %get-tuple-element.753.refs_0_, bf16[16,2816]{1,0:T(8,128)(2,1)S(1)} %collective-permute-done.27.refs_1_, ...), custom_call_target="tpu_custom_call", output_to_operand_aliasing={{2}: (4, {})} | custom-call | tf_op jit(solution)/shard_map/join/pallas_call | solution.py:283
  23.2 4.3 %collective-permute-start.30 = (bf16[64,2048]{1,0:T(8,128)(2,1)S(1)}, bf16[64,2048]{1,0:T(8,128)(2,1)S(1)}, u32[]{:S(2)}, u32[]{:S(2)}) collective-permute-start(bf16[64,2048]{1,0:T(8,128)(2,1)S(1)} %get-tuple-element.755.refs_1_), channel_id=1, source_target_pairs={{0,1},{1,0},{2,3},{3,2},{4,5},{5,4},{6,7},{7,6},{8,9},{9,8},{10,11... | collective-permute-start | bytes 786440 | tf_op jit(solution)/shard_map/ppermute | solution.py:42
  27.5 2.0 %merge0.1.refs_3_ = bf16[1,768,4096]{2,1,0:T(8,128)(2,1)} custom-call(bf16[768,4096]{1,0:T(8,128)(2,1)S(1)} %get-tuple-element.754.refs_0_, bf16[64,2048]{1,0:T(8,128)(2,1)S(1)} %get-tuple-element.755.refs_1_, bf16[768,64]{1,0:T(8,128)(2,1)S(1)} %get-tuple-element.756.refs_2_), custom_call_target="tpu_custom_call" | custom-call | flops 201326592 | bytes 3145728 | tf_op jit(solution)/shard_map/merge0/pallas_call | solution.py:302
  29.6 0.0 collective-permute-done.30.refs_1_
  29.6 2.0 %merge1.1 = bf16[1,768,4096]{2,1,0:T(8,128)(2,1)} custom-call(bf16[768,4096]{1,0:T(8,128)(2,1)S(1)} %get-tuple-element.754.refs_0_, bf16[64,2048]{1,0:T(8,128)(2,1)S(1)} %collective-permute-done.30.refs_1_, bf16[768,64]{1,0:T(8,128)(2,1)S(1)} %get-tuple-element.756.refs_2_, bf16[1,768,4096]{2,1,0:T(8,128)(2,1)} %merge0.1.refs_3_), custom_call_target="tpu_custom_call", output_to_operand_aliasing={{}: (3, {})} | custom-call | flops 201326592 | bytes 3145728 | tf_op jit(solution)/shard_map/merge1/pallas_call | solution.py:302
Async XLA Ops:
  1.8 5.8 %collective-permute-start.24 = (bf16[16,2816]{1,0:T(8,128)(2,1)S(1)}, bf16[16,2816]{1,0:T(8,128)(2,1)S(1)}, u32[]{:S(2)}, u32[]{:S(2)}) collective-permute-start(bf16[16,2816]{1,0:T(8,128)(2,1)S(1)} %get-tuple-element.750), channel_id=1, source_target_pairs={{0,8},{8,0},{16,24},{24,16},{1,9},{9,1},{17,25},{25,17},{2,10},{10... | collective-permute-start | bytes 270344 | tf_op jit(solution)/shard_map/ppermute | solution.py:42
  3.9 3.7 %collective-permute-start.25 = (bf16[16,2816]{1,0:T(8,128)(2,1)S(1)}, bf16[16,2816]{1,0:T(8,128)(2,1)S(1)}, u32[]{:S(2)}, u32[]{:S(2)}) collective-permute-start(bf16[16,2816]{1,0:T(8,128)(2,1)S(1)} %get-tuple-element.751), channel_id=1, source_target_pairs={{0,16},{8,24},{16,0},{24,8},{1,17},{9,25},{17,1},{25,9},{2,18},{10... | collective-permute-start | bytes 270344 | tf_op jit(solution)/shard_map/ppermute | solution.py:42
  5.1 4.4 %collective-permute-start.26 = (bf16[16,2816]{1,0:T(8,128)(2,1)S(1)}, bf16[16,2816]{1,0:T(8,128)(2,1)S(1)}, u32[]{:S(2)}, u32[]{:S(2)}) collective-permute-start(bf16[16,2816]{1,0:T(8,128)(2,1)S(1)} %get-tuple-element.752), channel_id=1, source_target_pairs={{0,24},{8,16},{16,8},{24,0},{1,25},{9,17},{17,9},{25,1},{2,26},{10... | collective-permute-start | bytes 270344 | tf_op jit(solution)/shard_map/ppermute | solution.py:42
  5.2 0.7 %copy-start = (s32[4]{0:T(128)S(1)}, s32[4]{0:T(128)}, u32[]{:S(2)}) copy-start(s32[4]{0:T(128)} %slot_of.1) | copy-start | bytes 52
  9.8 6.8 %collective-permute-start.19 = (bf16[16,2816]{1,0:T(8,128)(2,1)S(1)}, bf16[16,2816]{1,0:T(8,128)(2,1)}, u32[]{:S(2)}, u32[]{:S(2)}) collective-permute-start(bf16[16,2816]{1,0:T(8,128)(2,1)S(1)} %get-tuple-element.650), channel_id=1, source_target_pairs={{0,6},{2,0},{4,4},{6,2},{1,7},{3,1},{5,5},{7,3},{8,14},{10,8},{12,... | collective-permute-start | bytes 270344 | tf_op jit(solution)/shard_map/cond/branch_19_fun/ppermute | solution.py:241
  16.5 5.5 %collective-permute-start.29 = (bf16[16,2816]{1,0:T(8,128)(2,1)}, bf16[16,2816]{1,0:T(8,128)(2,1)S(1)}, u32[]{:S(2)}, u32[]{:S(2)}) collective-permute-start(bf16[16,2816]{1,0:T(8,128)(2,1)} %get-tuple-element.753.refs_0_), channel_id=1, source_target_pairs={{0,24},{8,16},{16,8},{24,0},{1,25},{9,17},{17,9},{25,1},{2,26},{10... | collective-permute-start | bytes 270344 | tf_op jit(solution)/shard_map/ppermute | solution.py:42
  17.4 4.6 %collective-permute-start.28 = (bf16[16,2816]{1,0:T(8,128)(2,1)}, bf16[16,2816]{1,0:T(8,128)(2,1)S(1)}, u32[]{:S(2)}, u32[]{:S(2)}) collective-permute-start(bf16[16,2816]{1,0:T(8,128)(2,1)} %get-tuple-element.753.refs_0_), channel_id=1, source_target_pairs={{0,16},{8,24},{16,0},{24,8},{1,17},{9,25},{17,1},{25,9},{2,18},{10... | collective-permute-start | bytes 270344 | tf_op jit(solution)/shard_map/ppermute | solution.py:42
  18.5 3.6 %collective-permute-start.27 = (bf16[16,2816]{1,0:T(8,128)(2,1)}, bf16[16,2816]{1,0:T(8,128)(2,1)S(1)}, u32[]{:S(2)}, u32[]{:S(2)}) collective-permute-start(bf16[16,2816]{1,0:T(8,128)(2,1)} %get-tuple-element.753.refs_0_), channel_id=1, source_target_pairs={{0,8},{8,0},{16,24},{24,16},{1,9},{9,1},{17,25},{25,17},{2,10},{10... | collective-permute-start | bytes 270344 | tf_op jit(solution)/shard_map/ppermute | solution.py:42
  23.2 6.4 %collective-permute-start.30 = (bf16[64,2048]{1,0:T(8,128)(2,1)S(1)}, bf16[64,2048]{1,0:T(8,128)(2,1)S(1)}, u32[]{:S(2)}, u32[]{:S(2)}) collective-permute-start(bf16[64,2048]{1,0:T(8,128)(2,1)S(1)} %get-tuple-element.755.refs_1_), channel_id=1, source_target_pairs={{0,1},{1,0},{2,3},{3,2},{4,5},{5,4},{6,7},{7,6},{8,9},{9,8},{10,11... | collective-permute-start | bytes 786440 | tf_op jit(solution)/shard_map/ppermute | solution.py:42

commit v4 on v3

v4 whole, which is shorter than its diff:
```python
import functools
import itertools

import jax
import jax.numpy as jnp
from jax import lax
from jax.experimental import pallas as pl
from jax.experimental.pallas import tpu as pltpu
from jax.sharding import PartitionSpec as P

ADAM_STEP = 20


ADAPTER_SCALE = 2.0
BETA_ONE = 0.9
BETA_TWO = 0.95
LEARN_RATE = 0.08
STABILITY_TERM = 1e-08

MOST_SWITCHED = 4

F32 = jnp.float32
BF16 = jnp.bfloat16
VMEM = pl.BlockSpec(memory_space=pltpu.VMEM)
SMEM = pl.BlockSpec(memory_space=pltpu.SMEM)
HBM = pl.BlockSpec(memory_space=pltpu.HBM)
PARAMS = pltpu.CompilerParams(vmem_limit_bytes=16 * 1024 * 1024)


def adam_update(param, moment, second, grad):
    corr_one = 1.0 - BETA_ONE**ADAM_STEP
    corr_two = 1.0 - BETA_TWO**ADAM_STEP
    moment_new = BETA_ONE * moment + (1.0 - BETA_ONE) * grad
    second_new = BETA_TWO * second + (1.0 - BETA_TWO) * grad * grad
    param_new = param - LEARN_RATE * (moment_new / corr_one) / (
        jnp.sqrt(second_new / corr_two) + STABILITY_TERM
    )
    return (param_new, moment_new, second_new)


def swap(x, axis, n, k):
    return lax.ppermute(x, axis, [(i, i ^ k) for i in range(n)])


def held(x):
    return pltpu.with_memory_space_constraint(x, pltpu.VMEM)


def left(x):
    return pltpu.with_memory_space_constraint(x, pltpu.HBM)


def estimate(nbytes, flops=0):
    return pl.CostEstimate(flops=flops, bytes_accessed=nbytes, transcendentals=0)


class Plan:
    def __init__(self, n, ranks, cols_a, cols_b):
        self.n, self.ranks, self.cols_a, self.cols_b = n, ranks, cols_a, cols_b
        cols = cols_a + cols_b
        middle = min(-(-cols // 256) * 128, cols_a)
        self.cols = cols
        self.spans = [(0, middle), (middle, cols)]
        self.widths = [middle, cols - middle]
        bits = [1 << i for i in range(n.bit_length() - 1)]
        self.orders = [bits, bits[::-1]]

    def split(self, half, step):
        blocks = list(range(self.n))
        for bit in self.orders[half][:step]:
            blocks = [k for k in blocks if not k & bit]
        bit = self.orders[half][step]
        return [k for k in blocks if k & bit], [k for k in blocks if not k & bit]

    def gathered(self, half, step):
        blocks = [0]
        for bit in self.orders[half][:step]:
            blocks = blocks + [k ^ bit for k in blocks]
        return blocks

    def pieces(self, half):
        low, high = self.spans[half]
        out = []
        if low < self.cols_a:
            out.append((False, low, min(high, self.cols_a), 0))
        if high > self.cols_a:
            start = max(low, self.cols_a)
            out.append((True, start - self.cols_a, high - self.cols_a, start - low))
        return out

    def grad_copies(self, grads, blocks, into, sems):
        me = lax.axis_index("dp")
        copies, at = [], 0
        for half in range(2):
            for i, k in enumerate(blocks[half]):
                rows = pl.ds(pl.multiple_of((me ^ k) * self.ranks, self.ranks), self.ranks)
                for is_b, start, stop, column in self.pieces(half):
                    copies.append(
                        pltpu.make_async_copy(
                            grads[is_b].at[0, 0, rows, pl.ds(start, stop - start)],
                            into[half].at[
                                pl.ds(i * self.ranks, self.ranks), pl.ds(column, stop - start)
                            ],
                            sems.at[at],
                        )
                    )
                    at += 1
        return copies

    def count(self, blocks):
        return sum(len(blocks[half]) * len(self.pieces(half)) for half in range(2))


def pack_kernel(plan, blocks, grad_a, grad_b, send0, send1, rows0, rows1, sems):
    copies = plan.grad_copies((grad_a, grad_b), blocks, (rows0, rows1), sems)
    for copy in copies:
        copy.start()
    for copy in copies:
        copy.wait()
    send0[...] = rows0[...].astype(BF16)
    send1[...] = rows1[...].astype(BF16)


def load_kernel(plan, blocks, *refs):
    slot_of, grad_a, grad_b, fa, fb, ma, mb, sa, sb = refs[:9]
    keep0, keep1, factor, moment, second, order, slots, sems, grad_sems = refs[9:]
    first = pl.ds(0, plan.cols_a)
    last = pl.ds(plan.cols_a, plan.cols_b)
    pairs = [
        (slot_of, slots),
        (fa.at[0], factor.at[:, first]),
        (fb.at[0], factor.at[:, last]),
        (ma.at[0], moment.at[:, first]),
        (mb.at[0], moment.at[:, last]),
        (sa.at[0], second.at[:, first]),
        (sb.at[0], second.at[:, last]),
    ]
    copies = [pltpu.make_async_copy(a, b, sems.at[i]) for i, (a, b) in enumerate(pairs)]
    copies += plan.grad_copies((grad_a, grad_b), blocks, (keep0, keep1), grad_sems)
    for copy in copies:
        copy.start()
    copies[0].wait()
    n = slots.shape[0]
    number = jnp.int32(0)
    if n <= MOST_SWITCHED:
        for i in range(n - 1):
            smaller = jnp.int32(0)
            for j in range(i + 1, n):
                smaller += (slots[j] < slots[i]).astype(jnp.int32)
            number = number * (n - i) + smaller
    order[0] = number
    for copy in copies[1:]:
        copy.wait()


def panel_kernel(k, chunks, weight, after, panel, sems):
    rows, cols = panel.shape
    at = pl.multiple_of((lax.axis_index("tensor") ^ k) * cols, cols)
    step = rows // chunks
    copies = [
        pltpu.make_async_copy(
            weight.at[0, pl.ds(i * step, step), pl.ds(at, cols)],
            panel.at[pl.ds(i * step, step), :],
            sems.at[i],
        )
        for i in range(chunks)
    ]
    for copy in copies:
        copy.start()
    for copy in copies:
        copy.wait()


def half_kernel(plan, step, *refs):
    r = plan.ranks
    for half in range(2):
        keep, got, send, kept = refs[half::2]
        total = keep[...] + got[...].astype(F32)
        blocks = plan.split(half, step - 1)[1]
        sent, stay = plan.split(half, step)
        rows = lambda ks: [total[blocks.index(k) * r : (blocks.index(k) + 1) * r] for k in ks]
        send[...] = jnp.concatenate(rows(sent), axis=0).astype(BF16)
        kept[...] = jnp.concatenate(rows(stay), axis=0)


def new_state(plan, refs):
    factor, moment, second = refs[:3]
    for half in range(2):
        keep, got = refs[3 + half], refs[5 + half]
        span = pl.ds(plan.spans[half][0], plan.widths[half])
        total = keep[...] + got[...].astype(F32)
        yield adam_update(factor[:, span], moment[:, span], second[:, span], total)


def send_kernel(plan, *refs):
    for half, new in enumerate(new_state(plan, refs[:7])):
        refs[8][:, pl.ds(plan.spans[half][0], plan.widths[half])] = new[0].astype(BF16)


def state_kernel(plan, *refs):
    outs = refs[7:]
    for half, new in enumerate(new_state(plan, refs[:7])):
        for is_b, start, stop, column in plan.pieces(half):
            for i, value in enumerate(new):
                outs[2 * i + is_b][0, :, pl.ds(start, stop - start)] = value[
                    :, column : column + stop - start
                ]


def stack_kernel(*refs):
    for half in range(2):
        held_rows, got, out = refs[half:6:2]
        rows = [held_rows[...].astype(F32), got[...].astype(F32)]
        out[...] = jnp.concatenate(rows, axis=0).astype(BF16)


def join_kernel(plan, *refs):
    rows_a, flipped = refs[4:]
    r = plan.ranks
    rows_b = None
    for half in range(2):
        rows = [ref[...].astype(F32) for ref in refs[half:4:2]]
        rows = jnp.concatenate(rows, axis=0)
        blocks = plan.gathered(half, len(plan.orders[half]))
        rows = [rows[blocks.index(k) * r : (blocks.index(k) + 1) * r] for k in range(plan.n)]
        rows = jnp.concatenate(rows, axis=0)
        for is_b, start, stop, column in plan.pieces(half):
            part = rows[:, column : column + stop - start]
            if is_b:
                flipped[...] = (part * ADAPTER_SCALE).T.astype(BF16)
            else:
                rows_a[:, start:stop] = part.astype(BF16)


def merge_kernel(k, width, *refs):
    panel, rows_a, flipped = refs[:3]
    out, tiles, sems = refs[-3:]
    cols = rows_a.shape[1]
    base = (lax.axis_index("tensor") ^ k) * cols
    copies = []
    for step in range(cols // width):
        span = slice(step * width, (step + 1) * width)
        increment = jnp.dot(flipped[...], rows_a[:, span], preferred_element_type=F32)
        tiles[step] = (panel[:, span].astype(F32) + increment).astype(BF16)
        columns = pl.ds(pl.multiple_of(base + step * width, width), width)
        copy = pltpu.make_async_copy(tiles.at[step], out.at[0, :, columns], sems.at[step])
        copy.start()
        copies.append(copy)
    for copy in copies:
        copy.wait()


def per_device(
    n_dp,
    n_expert,
    n_tensor,
    weight,
    factor_a,
    factor_b,
    moment_a,
    second_a,
    first_moment_factor_b,
    second_b,
    grad_a,
    grad_b,
    slot_of,
):
    ranks, cols_a = factor_a.shape[1:]
    cols_b = factor_b.shape[2]
    plan = Plan(n_dp, ranks, cols_a, cols_b)
    cols, widths = plan.cols, plan.widths
    steps = len(plan.orders[0])
    panel_shape = (weight.shape[1], cols_a)

    def load_panel(k, after):
        chunks = 8
        return held(
            pl.pallas_call(
                functools.partial(panel_kernel, k, chunks),
                in_specs=[HBM, VMEM],
                out_specs=VMEM,
                out_shape=pltpu.VMEM(panel_shape, BF16),
                scratch_shapes=[pltpu.SemaphoreType.DMA((chunks,))],
                compiler_params=PARAMS,
                cost_estimate=estimate(panel_shape[0] * cols_a * 4),
                name=f"panel{k}",
            )(left(weight), held(after))
        )

    sent = [plan.split(half, 0)[0] for half in range(2)]
    kept = [plan.split(half, 0)[1] for half in range(2)]
    shapes = [(len(sent[half]) * ranks, widths[half]) for half in range(2)]
    grads = (left(grad_a), left(grad_b))
    send = pl.pallas_call(
        functools.partial(pack_kernel, plan, sent),
        in_specs=[HBM, HBM],
        out_specs=[VMEM] * 2,
        out_shape=[pltpu.VMEM(shape, BF16) for shape in shapes],
        scratch_shapes=[pltpu.VMEM(shape, F32) for shape in shapes]
        + [pltpu.SemaphoreType.DMA((plan.count(sent),))],
        compiler_params=PARAMS,
        name="pack",
    )(*grads)
    got = [held(swap(send[half], "dp", n_dp, plan.orders[half][0])) for half in range(2)]
    *keep, factor, moment, second, order = pl.pallas_call(
        functools.partial(load_kernel, plan, kept),
        in_specs=[HBM] * 9,
        out_specs=[VMEM] * 5 + [SMEM],
        out_shape=[pltpu.VMEM(shape, F32) for shape in shapes]
        + [pltpu.VMEM((ranks, cols), F32)] * 3
        + [pltpu.SMEM((1,), jnp.int32)],
        scratch_shapes=[
            pltpu.SMEM(slot_of.shape, jnp.int32),
            pltpu.SemaphoreType.DMA((7,)),
            pltpu.SemaphoreType.DMA((plan.count(kept),)),
        ],
        compiler_params=PARAMS,
        cost_estimate=estimate(5 * ranks * cols * 4),
        name="load",
    )(
        left(slot_of),
        *grads,
        *map(
            left,
            (factor_a, factor_b, moment_a, first_moment_factor_b, second_a, second_b),
        ),
    )
    for step in range(1, steps):
        sent = [plan.split(half, step)[0] for half in range(2)]
        shapes = [(len(sent[half]) * ranks, widths[half]) for half in range(2)]
        *send, keep0, keep1 = pl.pallas_call(
            functools.partial(half_kernel, plan, step),
            in_specs=[VMEM] * 4,
            out_specs=[VMEM] * 4,
            out_shape=[pltpu.VMEM(shape, BF16) for shape in shapes]
            + [pltpu.VMEM(shape, F32) for shape in shapes],
            compiler_params=PARAMS,
            name=f"half{step}",
        )(*map(held, keep), *got)
        keep = [keep0, keep1]
        got = [held(swap(send[half], "dp", n_dp, plan.orders[half][step])) for half in range(2)]
    panel = load_panel(0, keep[0])
    state = [held(x) for x in (factor, moment, second, *keep)] + got

    send, panel = pl.pallas_call(
        functools.partial(send_kernel, plan),
        in_specs=[VMEM] * 8,
        out_specs=[VMEM] * 2,
        out_shape=[pltpu.VMEM((ranks, cols), BF16), pltpu.VMEM(panel_shape, BF16)],
        input_output_aliases={7: 1},
        compiler_params=PARAMS,
        name="send",
    )(*state, panel)

    def move(slots):
        def branch(send, state):
            mine = lax.ppermute(send, "expert", list(enumerate(slots)))
            new = pl.pallas_call(
                functools.partial(state_kernel, plan),
                in_specs=[VMEM] * 7,
                out_specs=[VMEM] * 6,
                out_shape=[
                    jax.ShapeDtypeStruct(factor_a.shape, F32),
                    jax.ShapeDtypeStruct(factor_b.shape, F32),
                ]
                * 3,
                compiler_params=PARAMS,
                cost_estimate=estimate(3 * ranks * cols * 4),
                name="state",
            )(*map(held, state))
            return [mine[:, low:high] for low, high in plan.spans], new

        return branch

    if n_expert <= MOST_SWITCHED:
        orders = list(itertools.permutations(range(n_expert)))
        mine, new = lax.switch(order[0], [move(slots) for slots in orders], send, state)
    else:
        mine, new = move(range(n_expert))(send, state)
        here = lax.axis_index("expert")
        experts = jnp.arange(n_expert, dtype=jnp.int32)
        wanted = jnp.sum(jnp.where(slot_of == here, experts, 0)) ^ here
        for k in range(1, n_expert):
            moved = swap(send, "expert", n_expert, k)
            mine = [
                jnp.where(wanted == k, moved[:, low:high], x)
                for x, (low, high) in zip(mine, plan.spans)
            ]
    new_a, new_b, new_moment_a, new_moment_b, new_second_a, new_second_b = new

    panels = [panel]
    for step in range(steps):
        got = [held(swap(mine[half], "dp", n_dp, plan.orders[half][step])) for half in range(2)]
        mine = [held(x) for x in mine]
        if step < steps - 1:
            rows = 2 * ranks << step
            mine = pl.pallas_call(
                stack_kernel,
                in_specs=[VMEM] * 4,
                out_specs=[VMEM] * 2,
                out_shape=[pltpu.VMEM((rows, widths[half]), BF16) for half in range(2)],
                compiler_params=PARAMS,
                name=f"stack{step}",
            )(*mine, *got)
    panels += [load_panel(k, mine[0]) for k in range(1, n_tensor)]
    rows_a, flipped, *panels = pl.pallas_call(
        functools.partial(join_passing, plan, n_tensor),
        in_specs=[VMEM] * (4 + n_tensor),
        out_specs=[VMEM] * (2 + n_tensor),
        out_shape=[
            pltpu.VMEM((ranks * n_dp, cols_a), BF16),
            pltpu.VMEM((cols_b, ranks * n_dp), BF16),
        ]
        + [pltpu.VMEM(panel_shape, BF16)] * n_tensor,
        input_output_aliases={4 + k: 2 + k for k in range(n_tensor)},
        compiler_params=PARAMS,
        name="join",
    )(*mine, *got, *map(held, panels))

    merged = None
    width = 512
    for k in range(n_tensor):
        block = held(rows_a if k == 0 else swap(rows_a, "tensor", n_tensor, k))
        operands = [held(panels[k]), block, held(flipped)] + ([] if merged is None else [merged])
        merged = pl.pallas_call(
            functools.partial(merge_kernel, k, width),
            in_specs=[VMEM] * 3 + [HBM] * (len(operands) - 3),
            out_specs=HBM,
            out_shape=jax.ShapeDtypeStruct(weight.shape, BF16),
            scratch_shapes=[
                pltpu.VMEM((cols_a // width, panel_shape[0], width), BF16),
                pltpu.SemaphoreType.DMA((cols_a // width,)),
            ],
            input_output_aliases={} if merged is None else {3: 0},
            compiler_params=PARAMS,
            cost_estimate=estimate(
                panel_shape[0] * cols_a * 2, 2 * panel_shape[0] * cols_a * ranks * n_dp
            ),
            name=f"merge{k}",
        )(*operands)
    return (merged, new_a, new_b, new_moment_a, new_second_a, new_moment_b, new_second_b)


def join_passing(plan, n_tensor, *refs):
    join_kernel(plan, *refs[:4], *refs[4 + n_tensor : 6 + n_tensor])


def solution(mesh):
    sizes = dict(mesh.shape)

    def body(*args):
        return per_device(sizes["dp"], sizes["expert"], sizes["tensor"], *args)

    state = P("expert", "dp", "tensor")
    grad = P("dp", "expert", None, "tensor")
    weight = P("expert", "tensor", None)
    in_specs = (weight,) + (state,) * 6 + (grad,) * 2 + (P(),)
    out_specs = (weight,) + (state,) * 6
    return jax.shard_map(body, mesh=mesh, in_specs=in_specs, out_specs=out_specs, check_vma=False)
```

time: 32.2 us -> 42.2 us (1.31); the launches traced: 31.6 us -> 42.2 us
  local copies, waits for them, and re-layouts: 0.65 us -> 7.63 us
  waiting for transfers between devices: 2.64 us -> 4.67 us
  starting transfers between devices: 15.6 us -> 17.6 us
    cond x0 -> x6, local copies, waits for them, and re-layouts: none -> 5.11 us
    ppermute x7 -> x9, starting transfers between devices: 10.4 us -> 13.4 us  [swap(): return lax.ppermute(x, axis, [(i, i ^ k) for i in range(n)])]
    ppermute x7 -> x9, waiting for transfers between devices: 2 us -> 4.67 us  [swap(): return lax.ppermute(x, axis, [(i, i ^ k) for i in range(n)])]
    unnamed x2 -> x16, local copies, waits for them, and re-layouts: 0.65 us -> 1.7 us
    ppermute x1, starting transfers between devices: 5.23 us -> 4.21 us  [branch(): mine = lax.ppermute(send, 'expert', list(enumerate(slots)))]
    slice x0 -> x1, local copies, waits for them, and re-layouts: none -> 0.82 us  [branch(): return ([mine[:, low:high] for low, high in plan.spans], new)]
    ppermute x1, waiting for transfers between devices: 0.63 us -> 0.01 us  [branch(): mine = lax.ppermute(send, 'expert', list(enumerate(slots)))]
    pallas_call x6 -> x9, Pallas kernels: 7.87 us -> 7.41 us  [the longest x2 3.81 us: load_panel(): pl.pallas_call(functools.partial(panel_kernel, k, chunks), in_specs=[HBM,...]
  transfers between devices with their start and end apart: 8 -> 10, of which waited for: 3 -> 5; matrix products, arithmetic and copies ran while one was open for 0% -> 12% of each run, Pallas kernels for 24% -> 19%
where the time goes in v4:
time: 42.2 us
  starting transfers between devices  17.6 us (42%)
  Pallas kernels  11.5 us (27%)
  local copies, waits for them, and re-layouts  7.63 us (18%)
  waiting for transfers between devices  4.67 us (11%)
  between operations  0.83 us (2%)
    ppermute x9, starting transfers between devices, swap(): return lax.ppermute(x, axis, [(i, i ^ k) for i in range(n)])  13.4 us
    cond x6, local copies, waits for them, and re-layouts  5.11 us
    ppermute x9, waiting for transfers between devices, swap(): return lax.ppermute(x, axis, [(i, i ^ k) for i in range(n)])  4.67 us
    ppermute x1, starting transfers between devices, branch(): mine = lax.ppermute(send, 'expert', list(enumerate(slots)))  4.21 us
    pallas_call x2, Pallas kernels, per_device(): pl.pallas_call(functools.partial(merge_kernel, k, width), in_specs=[VMEM]...  4.06 us
    pallas_call x2, Pallas kernels, load_panel(): pl.pallas_call(functools.partial(panel_kernel, k, chunks), in_specs=[HBM,...  3.81 us
    unnamed x16, local copies, waits for them, and re-layouts  1.7 us
    pallas_call x1, Pallas kernels, per_device(): pl.pallas_call(functools.partial(load_kernel, plan, kept), in_specs=[HBM]...  1.33 us
  transfers between devices with their start and end apart: 10, of which 5 were waited for; matrix products, arithmetic and copies ran while one was open for 12% of the time, Pallas kernels for 19%

profile of v4, /device:TPU:1, one launch (start us, length us, event | category | flops | bytes accessed | tf_op | source)
XLA Modules:
  0.0 42.2 jit_solution(9316547698349739178)
XLA Ops:
  0.6 1.0 %pack.1 = (bf16[32,1408]{1,0:T(8,128)(2,1)S(1)}, bf16[32,1408]{1,0:T(8,128)(2,1)S(1)}) custom-call(f32[1,1,64,2048]{3,2,1,0:T(8,128)} %grad_a.1, f32[1,1,64,768]{3,2,1,0:T(8,128)} %grad_b.1), custom_call_target="tpu_custom_call" | custom-call | tf_op jit(solution)/shard_map/pack/pallas_call | solution.py:294
  1.7 2.1 %collective-permute-start.24 = (bf16[32,1408]{1,0:T(8,128)(2,1)S(1)}, bf16[32,1408]{1,0:T(8,128)(2,1)S(1)}, u32[]{:S(2)}, u32[]{:S(2)}) collective-permute-start(bf16[32,1408]{1,0:T(8,128)(2,1)S(1)} %get-tuple-element.766), channel_id=1, source_target_pairs={{0,8},{8,0},{16,24},{24,16},{1,9},{9,1},{17,25},{25,17},{2,10},{10... | collective-permute-start | bytes 270344 | tf_op jit(solution)/shard_map/ppermute | solution.py:42
  3.8 1.2 %collective-permute-start.25 = (bf16[32,1408]{1,0:T(8,128)(2,1)S(1)}, bf16[32,1408]{1,0:T(8,128)(2,1)S(1)}, u32[]{:S(2)}, u32[]{:S(2)}) collective-permute-start(bf16[32,1408]{1,0:T(8,128)(2,1)S(1)} %get-tuple-element.767), channel_id=1, source_target_pairs={{0,16},{8,24},{16,0},{24,8},{1,17},{9,25},{17,1},{25,9},{2,18},{10... | collective-permute-start | bytes 270344 | tf_op jit(solution)/shard_map/ppermute | solution.py:42
  5.0 1.3 %load.1 = (f32[32,1408]{1,0:T(8,128)S(1)}, f32[32,1408]{1,0:T(8,128)S(1)}, f32[16,2816]{1,0:T(8,128)S(1)}, f32[16,2816]{1,0:T(8,128)S(1)}, f32[16,2816]{1,0:T(8,128)S(1)}, /*index=5*/s32[1]{0:T(128)S(4)}) custom-call(s32[4]{0:T(128)} %refs_0_.1, f32[1,1,64,2048]{3,2,1,0:T(8,128)} %grad_a.1, f32[1,1,64,768]{3,2,1,0:T(8,128)} %grad_b.1, ...), custom_call_target="tpu_custom_call" | custom-call | bytes 901120 | tf_op jit(solution)/shard_map/load/pallas_call | solution.py:305
  6.4 0.8 %collective-permute-done.25.refs_3_ = bf16[32,1408]{1,0:T(8,128)(2,1)S(1)} collective-permute-done((bf16[32,1408]{1,0:T(8,128)(2,1)S(1)}, bf16[32,1408]{1,0:T(8,128)(2,1)S(1)}, u32[]{:S(2)}, u32[]{:S(2)}) %collective-permute-start.25) | collective-permute-done | bytes 90144 | tf_op jit(solution)/shard_map/ppermute | solution.py:42
  7.2 1.5 %collective-permute-start.26 = (bf16[16,1408]{1,0:T(8,128)(2,1)S(1)}, bf16[16,1408]{1,0:T(8,128)(2,1)S(1)}, u32[]{:S(2)}, u32[]{:S(2)}) collective-permute-start(bf16[16,1408]{1,0:T(8,128)(2,1)S(1)} %get-tuple-element.770), channel_id=1, source_target_pairs={{0,16},{8,24},{16,0},{24,8},{1,17},{9,25},{17,1},{25,9},{2,18},{10... | collective-permute-start | bytes 135176 | tf_op jit(solution)/shard_map/ppermute | solution.py:42
  8.7 0.3 collective-permute-start.27
  9.0 1.9 %panel0.1.refs_7_ = bf16[768,2048]{1,0:T(8,128)(2,1)S(1)} custom-call(bf16[1,768,4096]{2,1,0:T(8,128)(2,1)} %weight.3, f32[16,1408]{1,0:T(8,128)S(1)} %get-tuple-element.768.after.refs_3_), custom_call_target="tpu_custom_call" | custom-call | bytes 6291456 | tf_op jit(solution)/shard_map/panel0/pallas_call | solution.py:278
  11.0 0.7 %collective-permute-done.27.refs_6_ = bf16[16,1408]{1,0:T(8,128)(2,1)S(1)} collective-permute-done((bf16[16,1408]{1,0:T(8,128)(2,1)S(1)}, bf16[16,1408]{1,0:T(8,128)(2,1)S(1)}, u32[]{:S(2)}, u32[]{:S(2)}) %collective-permute-start.27) | collective-permute-done | bytes 45088 | tf_op jit(solution)/shard_map/ppermute | solution.py:42
  11.6 0.2 send.1
  11.8 1.7 %copy-done = bf16[768,2048]{1,0:T(8,128)(2,1)} copy-done((bf16[768,2048]{1,0:T(8,128)(2,1)}, bf16[768,2048]{1,0:T(8,128)(2,1)S(1)}, u32[]{:S(2)}) %copy-start) | copy-done | bytes 3145752
  13.4 11.0 %conditional.1 = (bf16[16,2816]{1,0:T(8,128)(2,1)}, (f32[1,16,2048]{2,1,0:T(8,128)}, f32[1,16,768]{2,1,0:T(8,128)}, f32[1,16,2048]{2,1,0:T(8,128)}, f32[1,16,768...) conditional(s32[]{:T(128)} %bitcast, ...), branch_computations={%region_0.0_spmd, %region_1.0_spmd, %region_2.0_spmd, %region_3.0_... | conditional | bytes 2162816 | solution.py:377
  13.4 4.2 %collective-permute-start.14 = (bf16[16,2816]{1,0:T(8,128)(2,1)S(1)}, bf16[16,2816]{1,0:T(8,128)(2,1)}, u32[]{:S(2)}, u32[]{:S(2)}) collective-permute-start(bf16[16,2816]{1,0:T(8,128)(2,1)S(1)} %get-tuple-element.585), channel_id=1, source_target_pairs={{0,4},{2,2},{4,0},{6,6},{1,5},{3,3},{5,1},{7,7},{8,12},{10,10},{12... | collective-permute-start | bytes 270344 | tf_op jit(solution)/shard_map/cond/branch_14_fun/ppermute | solution.py:357
  17.7 0.9 %state.38 = (f32[1,16,2048]{2,1,0:T(8,128)}, f32[1,16,768]{2,1,0:T(8,128)}, f32[1,16,2048]{2,1,0:T(8,128)}, f32[1,16,768]{2,1,0:T(8,128)}, f32[1,16,2048]{2,1,0:T(8,128)}, /*index=5*/f32[1,16,768]{2,1,0:T(8,128)}) custom-call(f32[16,2816]{1,0:T(8,128)S(1)} %get-tuple-element.586.refs_0_, f32[16,2816]{1,0:T(8,128)S(1)} %get-tuple-element.587.refs_1_, ...), custom_call_target="tpu_custom_call" | custom-call | bytes 540672 | tf_op jit(solution)/shard_map/cond/branch_14_fun/state/pallas_call | solution.py:358
  18.5 0.8 %copy.244 = f32[1,16,768]{2,1,0:T(8,128)S(1)} copy(f32[1,16,768]{2,1,0:T(8,128)} %get-tuple-element.1099) | data formatting | bytes 98304 | tf_op jit(solution)/shard_map/cond
  19.3 0.8 %copy.240 = f32[1,16,768]{2,1,0:T(8,128)S(1)} copy(f32[1,16,768]{2,1,0:T(8,128)} %get-tuple-element.1095) | data formatting | bytes 98304 | tf_op jit(solution)/shard_map/cond
  20.1 0.8 %copy.242 = f32[1,16,768]{2,1,0:T(8,128)S(1)} copy(f32[1,16,768]{2,1,0:T(8,128)} %get-tuple-element.1097) | data formatting | bytes 98304 | tf_op jit(solution)/shard_map/cond
  20.9 0.9 %copy.239 = f32[1,16,2048]{2,1,0:T(8,128)S(1)} copy(f32[1,16,2048]{2,1,0:T(8,128)} %get-tuple-element.1094) | data formatting | bytes 262144 | tf_op jit(solution)/shard_map/cond
  21.8 0.9 %copy.241 = f32[1,16,2048]{2,1,0:T(8,128)S(1)} copy(f32[1,16,2048]{2,1,0:T(8,128)} %get-tuple-element.1096) | data formatting | bytes 262144 | tf_op jit(solution)/shard_map/cond
  22.7 0.9 %copy.243 = f32[1,16,2048]{2,1,0:T(8,128)S(1)} copy(f32[1,16,2048]{2,1,0:T(8,128)} %get-tuple-element.1098) | data formatting | bytes 262144 | tf_op jit(solution)/shard_map/cond
  23.6 0.8 %fusion.14 = (bf16[16,1408]{1,0:T(8,128)(2,1)S(1)}, bf16[16,1408]{1,0:T(8,128)(2,1)S(1)}) fusion(bf16[16,2816]{1,0:T(8,128)(2,1)} %collective-permute-done.14), kind=kLoop, calls=%fused_computation.14 | loop fusion | bytes 180224 | tf_op jit(solution)/shard_map/cond/branch_0_fun/slice | solution.py:371
  24.5 0.3 collective-permute-start.29
  24.8 0.5 %collective-permute-start.28 = (bf16[16,1408]{1,0:T(8,128)(2,1)S(1)}, bf16[16,1408]{1,0:T(8,128)(2,1)S(1)}, u32[]{:S(2)}, u32[]{:S(2)}) collective-permute-start(bf16[16,1408]{1,0:T(8,128)(2,1)S(1)} %get-tuple-element.797.refs_0_), channel_id=1, source_target_pairs={{0,8},{8,0},{16,24},{24,16},{1,9},{9,1},{17,25},{25,17},{2,10},{10... | collective-permute-start | bytes 135176 | tf_op jit(solution)/shard_map/ppermute | solution.py:42
  25.3 2.2 %collective-permute-done.29.refs_3_ = bf16[16,1408]{1,0:T(8,128)(2,1)S(1)} collective-permute-done((bf16[16,1408]{1,0:T(8,128)(2,1)S(1)}, bf16[16,1408]{1,0:T(8,128)(2,1)S(1)}, u32[]{:S(2)}, u32[]{:S(2)}) %collective-permute-start.29) | collective-permute-done | bytes 45088 | tf_op jit(solution)/shard_map/ppermute | solution.py:42
  27.5 0.2 collective-permute-done.28.refs_2_
  27.8 0.6 %collective-permute-start.31 = (bf16[32,1408]{1,0:T(8,128)(2,1)S(1)}, bf16[32,1408]{1,0:T(8,128)(2,1)S(1)}, u32[]{:S(2)}, u32[]{:S(2)}) collective-permute-start(bf16[32,1408]{1,0:T(8,128)(2,1)S(1)} %get-tuple-element.776.refs_1_), channel_id=1, source_target_pairs={{0,8},{8,0},{16,24},{24,16},{1,9},{9,1},{17,25},{25,17},{2,10},{10... | collective-permute-start | bytes 270344 | tf_op jit(solution)/shard_map/ppermute | solution.py:42
  28.3 1.2 %collective-permute-start.30 = (bf16[32,1408]{1,0:T(8,128)(2,1)S(1)}, bf16[32,1408]{1,0:T(8,128)(2,1)S(1)}, u32[]{:S(2)}, u32[]{:S(2)}) collective-permute-start(bf16[32,1408]{1,0:T(8,128)(2,1)S(1)} %get-tuple-element.775.after.refs_0_), channel_id=1, source_target_pairs={{0,16},{8,24},{16,0},{24,8},{1,17},{9,25},{17,1},{25,9},{2,18},{10... | collective-permute-start | bytes 270344 | tf_op jit(solution)/shard_map/ppermute | solution.py:42
  29.6 1.9 %panel1.1.refs_5_ = bf16[768,2048]{1,0:T(8,128)(2,1)S(1)} custom-call(bf16[1,768,4096]{2,1,0:T(8,128)(2,1)} %weight.3, bf16[32,1408]{1,0:T(8,128)(2,1)S(1)} %get-tuple-element.775.after.refs_0_), custom_call_target="tpu_custom_call" | custom-call | bytes 6291456 | tf_op jit(solution)/shard_map/panel1/pallas_call | solution.py:278
  31.6 0.8 %collective-permute-done.30.refs_2_ = bf16[32,1408]{1,0:T(8,128)(2,1)S(1)} collective-permute-done((bf16[32,1408]{1,0:T(8,128)(2,1)S(1)}, bf16[32,1408]{1,0:T(8,128)(2,1)S(1)}, u32[]{:S(2)}, u32[]{:S(2)}) %collective-permute-start.30) | collective-permute-done | bytes 90144 | tf_op jit(solution)/shard_map/ppermute | solution.py:42
  32.5 5.6 %collective-permute-start.32 = (bf16[64,2048]{1,0:T(8,128)(2,1)S(1)}, bf16[64,2048]{1,0:T(8,128)(2,1)S(1)}, u32[]{:S(2)}, u32[]{:S(2)}) collective-permute-start(bf16[64,2048]{1,0:T(8,128)(2,1)S(1)} %get-tuple-element.779.refs_1_), channel_id=1, source_target_pairs={{0,1},{1,0},{2,3},{3,2},{4,5},{5,4},{6,7},{7,6},{8,9},{9,8},{10,11... | collective-permute-start | bytes 786440 | tf_op jit(solution)/shard_map/ppermute | solution.py:42
  38.1 2.0 %merge0.1.refs_3_ = bf16[1,768,4096]{2,1,0:T(8,128)(2,1)} custom-call(bf16[768,2048]{1,0:T(8,128)(2,1)S(1)} %get-tuple-element.781.refs_0_, bf16[64,2048]{1,0:T(8,128)(2,1)S(1)} %get-tuple-element.779.refs_1_, bf16[768,64]{1,0:T(8,128)(2,1)S(1)} %get-tuple-element.780.refs_2_), custom_call_target="tpu_custom_call" | custom-call | flops 201326592 | bytes 3145728 | tf_op jit(solution)/shard_map/merge0/pallas_call | solution.py:425
  40.2 2.0 %merge1.1 = bf16[1,768,4096]{2,1,0:T(8,128)(2,1)} custom-call(bf16[768,2048]{1,0:T(8,128)(2,1)S(1)} %get-tuple-element.778.refs_0_, bf16[64,2048]{1,0:T(8,128)(2,1)S(1)} %collective-permute-done.32.refs_1_, bf16[768,64]{1,0:T(8,128)(2,1)S(1)} %get-tuple-element.780.refs_2_, bf16[1,768,4096]{2,1,0:T(8,128)(2,1)} %merge0.1.refs_3_), custom_call_target="tpu_custom_call", output_to_operand_aliasing={{}: (3, {})} | custom-call | flops 201326592 | bytes 3145728 | tf_op jit(solution)/shard_map/merge1/pallas_call | solution.py:425
  (23 shorter events, 0.3 us)
Async XLA Ops:
  1.7 4.7 %collective-permute-start.24 = (bf16[32,1408]{1,0:T(8,128)(2,1)S(1)}, bf16[32,1408]{1,0:T(8,128)(2,1)S(1)}, u32[]{:S(2)}, u32[]{:S(2)}) collective-permute-start(bf16[32,1408]{1,0:T(8,128)(2,1)S(1)} %get-tuple-element.766), channel_id=1, source_target_pairs={{0,8},{8,0},{16,24},{24,16},{1,9},{9,1},{17,25},{25,17},{2,10},{10... | collective-permute-start | bytes 270344 | tf_op jit(solution)/shard_map/ppermute | solution.py:42
  3.8 3.4 %collective-permute-start.25 = (bf16[32,1408]{1,0:T(8,128)(2,1)S(1)}, bf16[32,1408]{1,0:T(8,128)(2,1)S(1)}, u32[]{:S(2)}, u32[]{:S(2)}) collective-permute-start(bf16[32,1408]{1,0:T(8,128)(2,1)S(1)} %get-tuple-element.767), channel_id=1, source_target_pairs={{0,16},{8,24},{16,0},{24,8},{1,17},{9,25},{17,1},{25,9},{2,18},{10... | collective-permute-start | bytes 270344 | tf_op jit(solution)/shard_map/ppermute | solution.py:42
  7.2 3.8 %collective-permute-start.26 = (bf16[16,1408]{1,0:T(8,128)(2,1)S(1)}, bf16[16,1408]{1,0:T(8,128)(2,1)S(1)}, u32[]{:S(2)}, u32[]{:S(2)}) collective-permute-start(bf16[16,1408]{1,0:T(8,128)(2,1)S(1)} %get-tuple-element.770), channel_id=1, source_target_pairs={{0,16},{8,24},{16,0},{24,8},{1,17},{9,25},{17,1},{25,9},{2,18},{10... | collective-permute-start | bytes 135176 | tf_op jit(solution)/shard_map/ppermute | solution.py:42
  8.7 2.9 %collective-permute-start.27 = (bf16[16,1408]{1,0:T(8,128)(2,1)S(1)}, bf16[16,1408]{1,0:T(8,128)(2,1)S(1)}, u32[]{:S(2)}, u32[]{:S(2)}) collective-permute-start(bf16[16,1408]{1,0:T(8,128)(2,1)S(1)} %get-tuple-element.771), channel_id=1, source_target_pairs={{0,8},{8,0},{16,24},{24,16},{1,9},{9,1},{17,25},{25,17},{2,10},{10... | collective-permute-start | bytes 135176 | tf_op jit(solution)/shard_map/ppermute | solution.py:42
  11.8 1.7 %copy-start = (bf16[768,2048]{1,0:T(8,128)(2,1)}, bf16[768,2048]{1,0:T(8,128)(2,1)S(1)}, u32[]{:S(2)}) copy-start(bf16[768,2048]{1,0:T(8,128)(2,1)S(1)} %get-tuple-element.777.refs_4_) | copy-start | bytes 9437188
  13.4 10.2 %collective-permute-start.14 = (bf16[16,2816]{1,0:T(8,128)(2,1)S(1)}, bf16[16,2816]{1,0:T(8,128)(2,1)}, u32[]{:S(2)}, u32[]{:S(2)}) collective-permute-start(bf16[16,2816]{1,0:T(8,128)(2,1)S(1)} %get-tuple-element.585), channel_id=1, source_target_pairs={{0,4},{2,2},{4,0},{6,6},{1,5},{3,3},{5,1},{7,7},{8,12},{10,10},{12... | collective-permute-start | bytes 270344 | tf_op jit(solution)/shard_map/cond/branch_14_fun/ppermute | solution.py:357
  24.5 7.0 %copy-start.2 = (f32[1,16,2048]{2,1,0:T(8,128)}, f32[1,16,2048]{2,1,0:T(8,128)S(1)}, u32[]{:S(2)}) copy-start(f32[1,16,2048]{2,1,0:T(8,128)S(1)} %get-tuple-element.754) | copy-start | bytes 393220
  24.5 7.0 %copy-start.3 = (f32[1,16,2048]{2,1,0:T(8,128)}, f32[1,16,2048]{2,1,0:T(8,128)S(1)}, u32[]{:S(2)}) copy-start(f32[1,16,2048]{2,1,0:T(8,128)S(1)} %get-tuple-element.756) | copy-start | bytes 393220
  24.5 7.0 %copy-start.4 = (f32[1,16,2048]{2,1,0:T(8,128)}, f32[1,16,2048]{2,1,0:T(8,128)S(1)}, u32[]{:S(2)}) copy-start(f32[1,16,2048]{2,1,0:T(8,128)S(1)} %get-tuple-element.757) | copy-start | bytes 393220
  24.5 7.0 %copy-start.5 = (f32[1,16,768]{2,1,0:T(8,128)}, f32[1,16,768]{2,1,0:T(8,128)S(1)}, u32[]{:S(2)}) copy-start(f32[1,16,768]{2,1,0:T(8,128)S(1)} %get-tuple-element.759) | copy-start | bytes 147460
  24.5 7.0 %copy-start.6 = (f32[1,16,768]{2,1,0:T(8,128)}, f32[1,16,768]{2,1,0:T(8,128)S(1)}, u32[]{:S(2)}) copy-start(f32[1,16,768]{2,1,0:T(8,128)S(1)} %get-tuple-element.755) | copy-start | bytes 147460
  24.5 7.0 %copy-start.7 = (f32[1,16,768]{2,1,0:T(8,128)}, f32[1,16,768]{2,1,0:T(8,128)S(1)}, u32[]{:S(2)}) copy-start(f32[1,16,768]{2,1,0:T(8,128)S(1)} %get-tuple-element.758) | copy-start | bytes 147460
  24.5 3.0 %collective-permute-start.29 = (bf16[16,1408]{1,0:T(8,128)(2,1)S(1)}, bf16[16,1408]{1,0:T(8,128)(2,1)S(1)}, u32[]{:S(2)}, u32[]{:S(2)}) collective-permute-start(bf16[16,1408]{1,0:T(8,128)(2,1)S(1)} %get-tuple-element.798.refs_1_), channel_id=1, source_target_pairs={{0,16},{8,24},{16,0},{24,8},{1,17},{9,25},{17,1},{25,9},{2,18},{10... | collective-permute-start | bytes 135176 | tf_op jit(solution)/shard_map/ppermute | solution.py:42
  24.8 2.9 %collective-permute-start.28 = (bf16[16,1408]{1,0:T(8,128)(2,1)S(1)}, bf16[16,1408]{1,0:T(8,128)(2,1)S(1)}, u32[]{:S(2)}, u32[]{:S(2)}) collective-permute-start(bf16[16,1408]{1,0:T(8,128)(2,1)S(1)} %get-tuple-element.797.refs_0_), channel_id=1, source_target_pairs={{0,8},{8,0},{16,24},{24,16},{1,9},{9,1},{17,25},{25,17},{2,10},{10... | collective-permute-start | bytes 135176 | tf_op jit(solution)/shard_map/ppermute | solution.py:42
  27.8 3.8 %collective-permute-start.31 = (bf16[32,1408]{1,0:T(8,128)(2,1)S(1)}, bf16[32,1408]{1,0:T(8,128)(2,1)S(1)}, u32[]{:S(2)}, u32[]{:S(2)}) collective-permute-start(bf16[32,1408]{1,0:T(8,128)(2,1)S(1)} %get-tuple-element.776.refs_1_), channel_id=1, source_target_pairs={{0,8},{8,0},{16,24},{24,16},{1,9},{9,1},{17,25},{25,17},{2,10},{10... | collective-permute-start | bytes 270344 | tf_op jit(solution)/shard_map/ppermute | solution.py:42
  28.3 4.1 %copy-start.1 = (bf16[768,2048]{1,0:T(8,128)(2,1)S(1)}, bf16[768,2048]{1,0:T(8,128)(2,1)}, u32[]{:S(2)}) copy-start(bf16[768,2048]{1,0:T(8,128)(2,1)} %copy-done) | copy-start | bytes 9437188
  28.3 4.1 %collective-permute-start.30 = (bf16[32,1408]{1,0:T(8,128)(2,1)S(1)}, bf16[32,1408]{1,0:T(8,128)(2,1)S(1)}, u32[]{:S(2)}, u32[]{:S(2)}) collective-permute-start(bf16[32,1408]{1,0:T(8,128)(2,1)S(1)} %get-tuple-element.775.after.refs_0_), channel_id=1, source_target_pairs={{0,16},{8,24},{16,0},{24,8},{1,17},{9,25},{17,1},{25,9},{2,18},{10... | collective-permute-start | bytes 270344 | tf_op jit(solution)/shard_map/ppermute | solution.py:42
  32.5 7.7 %collective-permute-start.32 = (bf16[64,2048]{1,0:T(8,128)(2,1)S(1)}, bf16[64,2048]{1,0:T(8,128)(2,1)S(1)}, u32[]{:S(2)}, u32[]{:S(2)}) collective-permute-start(bf16[64,2048]{1,0:T(8,128)(2,1)S(1)} %get-tuple-element.779.refs_1_), channel_id=1, source_target_pairs={{0,1},{1,0},{2,3},{3,2},{4,5},{5,4},{6,7},{7,6},{8,9},{9,8},{10,11... | collective-permute-start | bytes 786440 | tf_op jit(solution)/shard_map/ppermute | solution.py:42
